TPU v7x, 512 devices: a whole 4x8x8 slice. The times are simulated.
512 devices in a mesh: dp: 32 (over x, y), tensor: 16 (over z, core).
Axes of the slice: x: 4, y: 8, z: 8, core: 2. Of those that a mesh axis runs over, the one named last changes fastest.
Arguments:
- tokens_in: bfloat16 [77824, 8192], P('dp', 'tensor'), may hold values from -6 to 6
- out_grad: bfloat16 [77824, 512], P(('dp', 'tensor')), may hold values from -0.125 to 0.125
- memory: float32 [32, 8192, 512], P('dp', 'tensor'), may hold values from -6 to 6
- right_init: float32 [512, 64], replicated, may hold values from -0.25 to 0.25
Outputs:
- left_factor: float32 [8192, 64], P('tensor')
- right_factor: float32 [512, 64], replicated
- new_memory: float32 [32, 8192, 512], P('dp', 'tensor')
All inputs are finite; a program needn't handle non-finite values.
Results may differ from a plain program's by a relative error of at most 0.0003.
Values may be sent and summed in bfloat16 or wider, within the bound.
No kernel may reach another device: no remote copies, remote signals or barrier semaphores. Data moves between devices by JAX's collectives and lax.ppermute only.
A program may use at most 64 MiB of HBM per device.

v0:
```python
import math

import jax
import jax.numpy as jnp
from jax import lax
from jax.sharding import PartitionSpec as P

ROWS = 8192
ITERS = 2


def contract_rows(slab, factor):
    return lax.dot_general(slab, factor, (((0,), (0,)), ((), ())), precision=lax.Precision.HIGHEST)


def right_solve(lower, matrix):
    return lax.linalg.triangular_solve(lower, matrix, left_side=False, lower=True, transpose_a=True)


def local_gram(left_raw):
    return jnp.dot(left_raw.T, left_raw, precision=lax.Precision.HIGHEST)


def normalize(left_raw):
    gram = lax.psum(local_gram(left_raw), "tensor")
    lower = jnp.linalg.cholesky(gram)
    return right_solve(lower, left_raw)


def on_device(tokens_in, out_grad, memory, right_init):
    replicas = lax.axis_size("dp")
    merged = memory[0] + lax.dot_general(
        tokens_in,
        lax.all_gather(out_grad, "tensor", axis=0, tiled=True),
        (((0,), (0,)), ((), ())),
        preferred_element_type=jnp.float32,
    )
    right = right_init
    left_hat = None
    for step in range(ITERS):
        local_left = jnp.dot(merged, right, precision=lax.Precision.HIGHEST)
        left_raw = lax.psum(local_left, "dp") / replicas
        left_hat = normalize(left_raw)
        partial_right = contract_rows(merged, left_hat)
        right = lax.psum(partial_right, ("dp", "tensor")) / replicas
    approx = jnp.dot(left_hat, right.T, precision=lax.Precision.HIGHEST)
    new_memory = (merged - approx)[None]
    return (math.sqrt(ROWS) * left_hat, right, new_memory)


def solution(mesh):
    return jax.shard_map(
        on_device,
        mesh=mesh,
        in_specs=(P("dp", "tensor"), P(("dp", "tensor"), None), P("dp", "tensor", None), P()),
        out_specs=(P("tensor", None), P(), P("dp", "tensor", None)),
        check_vma=False,
    )
```

profile of v0, /device:TPU:1, one launch (start us, length us, event | category | flops | bytes accessed | tf_op | source)
XLA Modules:
  0.0 1040.0 jit_solution(11263572707686578982)
XLA Ops:
  8.0 51.6 %all-gather.2.cloned.1.call-done = bf16[2432,512]{1,0:T(8,128)(2,1)} async-done(((bf16[152,512]{1,0:T(8,128)(2,1)}), bf16[2432,512]{1,0:T(8,128)(2,1)}) %all-gather.2.cloned.1.call-update) | async-done | bytes 2490384 | tf_op jit(solution)/shard_map/all_gather | solution.py:34
  59.6 3.5 convolution_add_fusion
  63.1 2.7 fusion.27
  65.9 146.0 %all-reduce.5.cloned.1.call-done = f32[512,64]{0,1:T(8,128)} async-done(((f32[512,64]{0,1:T(8,128)}), f32[512,64]{0,1:T(8,128)}) %all-reduce.5.cloned.1.call-update) | async-done | bytes 131088 | tf_op jit(solution)/shard_map/psum | solution.py:42
  211.9 1.9 fusion.7
  213.8 48.3 %psum.43 = f32[64,64]{0,1:T(8,128)} all-reduce(f32[64,64]{0,1:T(8,128)} %fusion.7), channel_id=1, replica_groups=mesh['dp'=32,'tensor'=16] {'tensor'}, use_global_device_ids=true, to_apply=%region_1.0 | all-reduce | flops 4096 | bytes 32768 | tf_op jit(solution)/shard_map/psum | solution.py:25
  262.0 1.5 copy.8
  264.9 7.2 cholesky.44
  273.5 2.0 fusion.14
  275.6 6.3 custom-call.6
  283.1 1.5 fusion.28
  284.6 262.7 %all-reduce.7.cloned.1.call-done = f32[512,64]{0,1:T(8,128)} async-done(((f32[512,64]{0,1:T(8,128)}), f32[512,64]{0,1:T(8,128)}) %all-reduce.7.cloned.1.call-update) | async-done | bytes 131088 | tf_op jit(solution)/shard_map/psum | solution.py:45
  547.3 2.7 fusion.1
  550.1 142.7 %all-reduce.9.cloned.1.call-done = f32[512,64]{0,1:T(8,128)} async-done(((f32[512,64]{0,1:T(8,128)}), f32[512,64]{0,1:T(8,128)}) %all-reduce.9.cloned.1.call-update) | async-done | bytes 131088 | tf_op jit(solution)/shard_map/psum | solution.py:42
  692.8 1.9 fusion.4
  694.7 48.3 %psum.46 = f32[64,64]{0,1:T(8,128)} all-reduce(f32[64,64]{0,1:T(8,128)} %fusion.4), channel_id=1, replica_groups=mesh['dp'=32,'tensor'=16] {'tensor'}, use_global_device_ids=true, to_apply=%region_6.9 | all-reduce | flops 4096 | bytes 32768 | tf_op jit(solution)/shard_map/psum | solution.py:25
  743.0 1.5 copy.10
  745.8 7.2 cholesky.55
  754.5 2.0 fusion.15
  756.5 6.3 custom-call.7
  762.8 1.9 broadcast_multiply_fusion
  765.3 1.5 fusion.29
  766.8 262.8 %all-reduce.11.cloned.1.call-done = f32[512,64]{0,1:T(8,128)} async-done(((f32[512,64]{0,1:T(8,128)}), f32[512,64]{0,1:T(8,128)}) %all-reduce.11.cloned.1.call-update) | async-done | bytes 131088 | tf_op jit(solution)/shard_map/psum | solution.py:45
  1030.6 3.0 fusion
  (24 shorter events, 9.4 us)
Async XLA Ops:
  7.2 52.4 %copy-start = (bf16[2432,512]{1,0:T(8,128)(2,1)S(1)}, bf16[2432,512]{1,0:T(8,128)(2,1)}, u32[]{:S(2)}) copy-start(bf16[2432,512]{1,0:T(8,128)(2,1)} %param.7) | copy-start | bytes 7471108
  7.2 52.4 %all-gather.2.cloned.1.call-start = ((), (), s32[]{:S(2)}) async-start(), calls=%async_computation | async-start | bytes 2646016 | tf_op jit(solution)/shard_map/all_gather | solution.py:34
  7.9 204.0 %all-reduce.5.cloned.1.call-start = ((), (), s32[]{:S(2)}) async-start(), calls=%async_computation.1 | async-start | bytes 262144 | tf_op jit(solution)/shard_map/psum | solution.py:42
  65.9 481.5 %all-reduce.7.cloned.1.call-start = ((), (), s32[]{:S(2)}) async-start(), calls=%async_computation.2 | async-start | bytes 262144 | tf_op jit(solution)/shard_map/psum | solution.py:45
  284.6 408.3 %all-reduce.9.cloned.1.call-start = ((), (), s32[]{:S(2)}) async-start(), calls=%async_computation.3 | async-start | bytes 262144 | tf_op jit(solution)/shard_map/psum | solution.py:42
  550.0 479.6 %all-reduce.11.cloned.1.call-start = ((), (), s32[]{:S(2)}) async-start(), calls=%async_computation.4 | async-start | bytes 262144 | tf_op jit(solution)/shard_map/psum | solution.py:45
  764.7 0.6 copy-start.1
  1030.5 3.0 copy-start.2
Sparse Core Ops, SparseCore 0:
  10.1 49.4 all-gather.1
  66.0 145.8 all-reduce.4
  284.7 262.5 all-reduce.6
  551.2 141.5 all-reduce.8
  766.9 262.6 all-reduce.10
where the time goes:
time: 1040 us
  waiting for transfers between devices  867 us (83%)
  blocking collectives  96.5 us (9%)
  other arithmetic  37.6 us (4%)
  matrix products  21.6 us (2%)
  between operations  13.8 us (1%)
    psum x2, waiting for transfers between devices, on_device(): right = lax.psum(partial_right, ('dp', 'tensor')) / replicas  526 us
    psum x2, waiting for transfers between devices, on_device(): left_raw = lax.psum(local_left, 'dp') / replicas  289 us
    psum x2, blocking collectives, normalize(): gram = lax.psum(local_gram(left_raw), 'tensor')  96.5 us
    all_gather x1, waiting for transfers between devices, on_device(): lax.all_gather(out_grad, 'tensor', axis=0, tiled=True)  51.6 us
  transfers between devices with their start and end apart: 5, of which 5 were waited for; matrix products, arithmetic and copies ran while one was open for 0% of the time, Pallas kernels for 0%

commit v1 on v0

v1 whole, which is shorter than its diff:
```python
import math

import jax
import jax.numpy as jnp
from jax import lax
from jax.sharding import PartitionSpec as P

ROWS = 8192
RANK = 64
HIGH = lax.Precision.HIGHEST


def dot(a, b, ca, cb):
    return lax.dot_general(a, b, (((ca,), (cb,)), ((), ())), precision=HIGH, preferred_element_type=jnp.float32)


def exchange(pieces, axis):
    return lax.all_to_all(pieces, axis, 0, 0, tiled=False)


def fan_out(piece, axis):
    return exchange(jnp.broadcast_to(piece[None], (lax.axis_size(axis),) + piece.shape), axis)


def inverse_factor(gram):
    lower = jnp.linalg.cholesky(gram)
    eye = jnp.eye(RANK, dtype=jnp.float32)
    return lax.linalg.triangular_solve(lower, eye, left_side=True, lower=True)


def second_moment_rows(mean_slab, position):
    q, h = position // 2, position % 2
    first = h * 128 + 8 * q
    second = jnp.where(h == 1, 256, 384) + 8 * q
    step = lax.broadcasted_iota(jnp.int32, (16, 512), 0)
    wanted = jnp.where(step < 8, first + step, second + step - 8)
    pick = (lax.broadcasted_iota(jnp.int32, (16, 512), 1) == wanted).astype(jnp.float32)
    rows = dot(dot(pick, mean_slab, 1, 1), mean_slab, 1, 0)
    low = jnp.concatenate([rows[:8, :512], rows[8:, 384:]], axis=1)
    high = jnp.concatenate([rows[:8, 128:], rows[8:, 256:]], axis=1)
    return jnp.where(h == 1, high, low)


def assemble(tiles):
    tiles = tiles.reshape(16, 2, 8, 640)

    def block(h, t):
        return tiles[:, h, :, 128 * t : 128 * t + 128].reshape(128, 128)

    upper = {
        (0, 0): block(0, 0), (0, 1): block(0, 1), (0, 2): block(0, 2), (0, 3): block(0, 3),
        (1, 1): block(1, 0), (1, 2): block(1, 1), (1, 3): block(1, 2),
        (2, 2): block(1, 3), (2, 3): block(1, 4), (3, 3): block(0, 4),
    }
    return jnp.concatenate(
        [
            jnp.concatenate([upper[i, j] if i <= j else upper[j, i].T for j in range(4)], axis=1)
            for i in range(4)
        ],
        axis=0,
    )


def on_device(tokens_in, out_grad, memory, right_init):
    replicas = lax.axis_size("dp")
    merged = memory[0] + lax.dot_general(
        tokens_in,
        lax.all_gather(out_grad, "tensor", axis=0, tiled=True),
        (((0,), (0,)), ((), ())),
        preferred_element_type=jnp.float32,
    )
    mean_rows = jnp.sum(exchange(merged.reshape(replicas, -1, 512), "dp"), axis=0) / replicas
    mean_slab = fan_out(mean_rows, "dp").reshape(512, 512)
    tiles = second_moment_rows(mean_slab, lax.axis_index("dp"))
    tiles = jnp.sum(fan_out(tiles, "tensor"), axis=0)
    moment = assemble(fan_out(tiles, "dp"))

    image = dot(moment, right_init, 1, 0)
    right = dot(image, inverse_factor(dot(right_init, image, 0, 0)), 1, 1)
    image = dot(moment, right, 1, 0)
    inverse = inverse_factor(dot(right, image, 0, 0))
    left_hat = dot(dot(mean_slab, right, 1, 0), inverse, 1, 1)
    right = dot(image, inverse, 1, 1)
    new_memory = (merged - dot(left_hat, right, 1, 1))[None]
    return (math.sqrt(ROWS) * left_hat, right, new_memory)


def solution(mesh):
    return jax.shard_map(
        on_device,
        mesh=mesh,
        in_specs=(P("dp", "tensor"), P(("dp", "tensor"), None), P("dp", "tensor", None), P()),
        out_specs=(P("tensor", None), P(), P("dp", "tensor", None)),
        check_vma=False,
    )
```

time: 1040 us -> 253 us (0.24)
  waiting for transfers between devices: 867 us -> 77.1 us
  blocking collectives: 96.5 us -> 79.9 us
  local copies, waits for them, and re-layouts: 3.56 us -> 16.3 us
    psum x4 -> x0, waiting for transfers between devices: 814 us -> none  [the longest x2 526 us: on_device(): right = lax.psum(partial_right, ('dp', 'tensor')) / replicas]
    psum x2 -> x0, blocking collectives: 96.5 us -> none  [normalize(): gram = lax.psum(local_gram(left_raw), 'tensor')]
    all_to_all x0 -> x3, blocking collectives: none -> 79.9 us  [exchange(): return lax.all_to_all(pieces, axis, 0, 0, tiled=False)]
    all_to_all x0 -> x1, waiting for transfers between devices: none -> 24.8 us  [exchange(): return lax.all_to_all(pieces, axis, 0, 0, tiled=False)]
  transfers between devices with their start and end apart: 5 -> 2, of which waited for: 5 -> 2; matrix products, arithmetic and copies ran while one was open for 0% -> 0% of each run, Pallas kernels for 0% -> 0%
where the time goes in v1:
time: 253 us; the launch traced here: 251 us
  blocking collectives  79.9 us (32%)
  waiting for transfers between devices  77.1 us (30%)
  other arithmetic  34.8 us (14%)
  matrix products  20.8 us (8%)
  local copies, waits for them, and re-layouts  16.3 us (6%)
  between operations  14.3 us (6%)
  starting transfers between devices  8.15 us (3%)
    all_to_all x3, blocking collectives, exchange(): return lax.all_to_all(pieces, axis, 0, 0, tiled=False)  79.9 us
    all_gather x1, waiting for transfers between devices, on_device(): lax.all_gather(out_grad, 'tensor', axis=0, tiled=True)  51.7 us
    all_to_all x1, waiting for transfers between devices, exchange(): return lax.all_to_all(pieces, axis, 0, 0, tiled=False)  24.8 us
    dot_general x11, matrix products, dot(): lax.dot_general(a, b, (((ca,), (cb,)), ((), ())), precision=HIGH, preferr...  16.1 us
    another operation x6, other arithmetic, inverse_factor(): lower = jnp.linalg.cholesky(gram)  15.2 us
    another operation x4, other arithmetic, inverse_factor(): return lax.linalg.triangular_solve(lower, eye, left_side=True, lower=True)  13.8 us
    all_to_all x1, starting transfers between devices, exchange(): return lax.all_to_all(pieces, axis, 0, 0, tiled=False)  8.11 us
    another operation x4, local copies, waits for them, and re-layouts, block(): return tiles[:, h, :, 128 * t:128 * t + 128].reshape(128, 128)  5.57 us
  transfers between devices with their start and end apart: 2, of which 2 were waited for; matrix products, arithmetic and copies ran while one was open for 0% of the time, Pallas kernels for 0%

profile of v1, /device:TPU:1, one launch (start us, length us, event | category | flops | bytes accessed | tf_op | source)
XLA Modules:
  0.0 251.4 jit_solution(12190651191943826984)
XLA Ops:
  7.9 51.7 %all-gather.2.cloned.1.call-done = bf16[2432,512]{1,0:T(8,128)(2,1)} async-done(((bf16[152,512]{1,0:T(8,128)(2,1)}), bf16[2432,512]{1,0:T(8,128)(2,1)}) %all-gather.2.cloned.1.call-update) | async-done | bytes 2490384 | tf_op jit(solution)/shard_map/all_gather | solution.py:68
  59.6 3.5 %convolution_add_fusion = f32[512,512]{1,0:T(8,128)S(1)} fusion(bf16[2432,512]{1,0:T(8,128)(2,1)S(1)} %copy-done, bf16[2432,512]{1,0:T(8,128)(2,1)} %all-gather.2.cloned.1.call-done, f32[1,512,512]{2,1,0:T(8,128)} %param.9), kind=kOutput, calls=%fused_computation.2 | convolution fusion | flops 1275330560 | bytes 7077888 | tf_op jit(solution)/shard_map/dot_general | solution.py:66
  64.1 34.2 %all_to_all.20 = f32[32,16,512]{2,1,0:T(8,128)S(1)} all-to-all(f32[32,16,512]{2,1,0:T(8,128)S(1)} %bitcast.82), channel_id=1, replica_groups=mesh['dp'=32,'tensor'=16] {'dp'}, dimensions={0} | all-to-all | bytes 2097152 | tf_op jit(solution)/shard_map/all_to_all | solution.py:18
  100.9 8.1 %all-to-all-start.1 = ((f32[32,16,512]{2,1,0:T(8,128)}), f32[32,16,512]{2,1,0:T(8,128)S(1)}, u32[]{:S(2)}, u32[]{:S(2)}) async-start(f32[32,16,512]{2,1,0:T(8,128)} %broadcast_in_dim.8), calls=%async_computation.1 | async-start | bytes 2097152 | tf_op jit(solution)/shard_map/all_to_all | solution.py:18
  109.1 24.8 %all-to-all-done.1 = f32[32,16,512]{2,1,0:T(8,128)S(1)} async-done(((f32[32,16,512]{2,1,0:T(8,128)}), f32[32,16,512]{2,1,0:T(8,128)S(1)}, u32[]{:S(2)}, u32[]{:S(2)}) %all-to-all-start.1) | async-done | bytes 1048608 | tf_op jit(solution)/shard_map/all_to_all | solution.py:18
  135.1 22.1 %all_to_all.21 = f32[16,8,640]{2,1,0:T(8,128)} all-to-all(f32[16,8,640]{2,1,0:T(8,128)S(1)} %broadcast_in_dim.9), channel_id=1, replica_groups=mesh['dp'=32,'tensor'=16] {'tensor'}, dimensions={0} | all-to-all | bytes 655360 | tf_op jit(solution)/shard_map/all_to_all | solution.py:18
  157.2 1.6 reduce_sum.19
  159.6 23.6 %all_to_all.22 = f32[32,8,640]{2,1,0:T(8,128)S(1)} all-to-all(f32[32,8,640]{2,1,0:T(8,128)S(1)} %broadcast_in_dim.10), channel_id=1, replica_groups=mesh['dp'=32,'tensor'=16] {'dp'}, dimensions={0} | all-to-all | bytes 1310720 | tf_op jit(solution)/shard_map/all_to_all | solution.py:18
  184.0 1.6 copy.18
  185.6 1.6 copy.19
  187.2 1.6 copy.20
  188.7 1.6 copy.17
  190.3 1.6 copy.16
  191.8 1.6 copy.15
  195.7 2.0 fusion.15
  202.1 7.2 %cholesky.44 = f32[64,64]{1,0:T(8,128)} custom-call(f32[64,64]{1,0:T(8,128)} %add_multiply_fusion), custom_call_target="Cholesky" | custom-call | tf_op jit(solution)/shard_map/jit(cholesky)/cholesky | solution.py:26
  210.8 2.0 fusion.5
  212.8 6.3 %custom-call.6 = f32[1,64,64]{1,2,0:T(8,128)} custom-call(f32[1,64,64]{2,1,0:T(8,128)} %fusion.5), custom_call_target="InvertDiagBlocksLowerTriangular" | custom-call | tf_op jit(solution)/shard_map/triangular_solve/custom-call.0 | solution.py:28
  221.3 2.4 fusion.19
  223.6 1.7 fusion.18
  225.7 5.8 %cholesky.55 = f32[64,64]{1,0:T(8,128)S(1)} custom-call(f32[64,64]{1,0:T(8,128)S(1)} %fusion.8), custom_call_target="Cholesky" | custom-call | tf_op jit(solution)/shard_map/jit(cholesky)/cholesky | solution.py:26
  232.8 4.9 %custom-call.7 = f32[1,64,64]{1,2,0:T(8,128)S(1)} custom-call(f32[1,64,64]{2,1,0:T(8,128)S(1)} %fusion.6), custom_call_target="InvertDiagBlocksLowerTriangular" | custom-call | tf_op jit(solution)/shard_map/triangular_solve/custom-call.0 | solution.py:28
  239.2 2.1 broadcast_multiply_fusion
  241.3 3.2 %fusion = f32[1,512,512]{2,1,0:T(8,128)} fusion(f32[512,512]{1,0:T(8,128)} %copy-done.2, f32[512,64]{0,1:T(8,128)S(1)} %get-tuple-element.19, f32[512,64]{0,1:T(8,128)S(1)} %fusion.21), kind=kOutput, calls=%fused_computation.1 | convolution fusion | flops 201588736 | bytes 2359296 | tf_op jit(solution)/shard_map/dot_general | solution.py:14
  (47 shorter events, 20.5 us)
Async XLA Ops:
  7.2 52.4 %copy-start = (bf16[2432,512]{1,0:T(8,128)(2,1)S(1)}, bf16[2432,512]{1,0:T(8,128)(2,1)}, u32[]{:S(2)}) copy-start(bf16[2432,512]{1,0:T(8,128)(2,1)} %param.7) | copy-start | bytes 7471108
  7.2 52.4 %all-gather.2.cloned.1.call-start = ((), (), s32[]{:S(2)}) async-start(), calls=%async_computation.4 | async-start | bytes 2646016 | tf_op jit(solution)/shard_map/all_gather | solution.py:68
  63.1 1.0 copy-start.2
  100.9 32.9 %all-to-all-start.1 = ((f32[32,16,512]{2,1,0:T(8,128)}), f32[32,16,512]{2,1,0:T(8,128)S(1)}, u32[]{:S(2)}, u32[]{:S(2)}) async-start(f32[32,16,512]{2,1,0:T(8,128)} %broadcast_in_dim.8), calls=%async_computation.1 | async-start | bytes 2097152 | tf_op jit(solution)/shard_map/all_to_all | solution.py:18
  193.4 5.0 %copy-start.5 = (f32[512,64]{0,1:T(8,128)S(1)}, f32[512,64]{0,1:T(8,128)}, u32[]{:S(2)}) copy-start(f32[512,64]{0,1:T(8,128)} %param.10) | copy-start | bytes 393220
  194.7 1.0 copy-start.1
  197.8 0.7 copy-start.4
  223.6 1.7 copy-start.3
  239.2 5.3 %copy-start.6 = (f32[512,64]{0,1:T(8,128)}, f32[512,64]{0,1:T(8,128)S(1)}, u32[]{:S(2)}) copy-start(f32[512,64]{0,1:T(8,128)S(1)} %fusion.21) | copy-start | bytes 393220
Sparse Core Ops, SparseCore 0:
  10.1 49.4 all-gather.1

commit v2 on v0

v2 whole, which is shorter than its diff:
```python
import math

import jax
import jax.numpy as jnp
from jax import lax
from jax.experimental import pallas as pl
from jax.experimental.pallas import tpu as pltpu
from jax.sharding import PartitionSpec as P

ROWS, COLS, RANK = 8192, 512, 64
F32 = jnp.float32
PARAMS = pltpu.CompilerParams(vmem_limit_bytes=32 * 1024 * 1024)


def dot(a, b, ca, cb):
    return lax.dot_general(
        a, b, (((ca,), (cb,)), ((), ())), precision=lax.Precision.HIGHEST, preferred_element_type=F32
    )


def shape(*dims):
    return jax.ShapeDtypeStruct(dims, F32)


def exchange(pieces, axis):
    return lax.all_to_all(pieces, axis, 0, 0, tiled=False)


def mean_kernel(parts_ref, copies_ref):
    count = parts_ref.shape[0]
    mean = jnp.sum(parts_ref[...], axis=0) * (1.0 / count)
    copies_ref[...] = jnp.broadcast_to(mean[None], copies_ref.shape)


def moment_kernel(slab_ref, copies_ref):
    position = lax.axis_index("dp")
    offset = 8 * lax.div(position, 2)
    odd = lax.rem(position, 2) == 1
    first = jnp.where(odd, 128, 0) + offset
    second = jnp.where(odd, 256, 384) + offset - 8
    step = lax.broadcasted_iota(jnp.int32, (16, COLS), 0)
    wanted = step + jnp.where(step < 8, first, second)
    pick = jnp.where(lax.broadcasted_iota(jnp.int32, (16, COLS), 1) == wanted, 1.0, 0.0)
    slab = slab_ref[...]
    rows = dot(dot(pick, slab, 1, 1), slab, 1, 0)
    low = jnp.concatenate([rows[:8, :], rows[8:, 384:]], axis=1)
    high = jnp.concatenate([rows[:8, 128:], rows[8:, 256:]], axis=1)
    tiles = jnp.where(odd, high, low)
    copies_ref[...] = jnp.broadcast_to(tiles[None], copies_ref.shape)


def sum_kernel(parts_ref, copies_ref):
    total = jnp.sum(parts_ref[...], axis=0)
    copies_ref[...] = jnp.broadcast_to(total[None], copies_ref.shape)


def inverse_factor(gram):
    lane = lax.broadcasted_iota(jnp.int32, (8, 128), 1)
    row = lax.broadcasted_iota(jnp.int32, (8, 128), 0)
    blocks = []
    for b in range(8):
        wide = jnp.concatenate([gram[8 * b : 8 * b + 8], jnp.zeros((8, RANK), F32)], axis=1)
        blocks.append(jnp.where(lane == RANK + 8 * b + row, 1.0, wide))
    for k in range(RANK):
        own, r = divmod(k, 8)
        pivot_row = jnp.broadcast_to(blocks[own][r : r + 1], (8, 128))
        scale = lax.rsqrt(jnp.broadcast_to(pivot_row[:, k : k + 1], (8, 128)))
        scaled = pivot_row * scale
        for b in range(own, 8):
            new = blocks[b] - jnp.broadcast_to(blocks[b][:, k : k + 1], (8, 128)) * scale * scaled
            if b == own:
                new = jnp.where(row > r, new, jnp.where(row == r, scaled, blocks[b]))
            blocks[b] = new
    return jnp.concatenate([block[:, RANK:] for block in blocks], axis=0)


def final_kernel(tiles_ref, slab_ref, merged_ref, right_ref, left_out, right_out, memory_out, moment):
    places = {(i, j): (i, j - i) for i in range(2) for j in range(i, 4)}
    places |= {(2, 2): (1, 3), (2, 3): (1, 4), (3, 3): (0, 4)}
    for (i, j), (h, t) in places.items():
        block = tiles_ref[:, h, :, 128 * t : 128 * t + 128].reshape(128, 128)
        moment[128 * i : 128 * i + 128, 128 * j : 128 * j + 128] = block
        if i != j:
            moment[128 * j : 128 * j + 128, 128 * i : 128 * i + 128] = block.T
    start = right_ref[...]
    image = dot(start, moment[...], 1, 0)
    right = dot(inverse_factor(dot(start, image, 1, 1)), image, 1, 0)
    image = dot(right, moment[...], 1, 0)
    left_raw = dot(right, slab_ref[...], 1, 1)
    inverse = inverse_factor(dot(right, image, 1, 1))
    left = dot(inverse, left_raw, 1, 0)
    right = dot(inverse, image, 1, 0)
    left_out[...] = math.sqrt(ROWS) * left
    right_out[...] = right
    memory_out[...] = merged_ref[...] - dot(left, right, 0, 0)


def call(kernel, out_shape, flops, moved, scratch=()):
    return pl.pallas_call(
        kernel,
        out_shape=out_shape,
        scratch_shapes=scratch,
        compiler_params=PARAMS,
        cost_estimate=pl.CostEstimate(flops=flops, bytes_accessed=moved, transcendentals=0),
    )


def on_device(tokens_in, out_grad, memory, right_init):
    replicas, pieces = lax.axis_size("dp"), lax.axis_size("tensor")
    merged = memory[0] + lax.dot_general(
        tokens_in,
        lax.all_gather(out_grad, "tensor", axis=0, tiled=True),
        (((0,), (0,)), ((), ())),
        preferred_element_type=F32,
    )
    parts = exchange(merged.reshape(replicas, -1, COLS), "dp")
    copies = call(mean_kernel, shape(32, 16, COLS), 1 << 18, 1 << 21)(parts)
    slab = exchange(copies, "dp").reshape(COLS, COLS)
    copies = call(moment_kernel, shape(pieces, 8, 640), 1 << 26, 1 << 20)(slab)
    copies = call(sum_kernel, shape(replicas, 8, 640), 1 << 17, 1 << 20)(exchange(copies, "tensor"))
    tiles = exchange(copies, "dp").reshape(16, 2, 8, 640)
    left, right, new_memory = call(
        final_kernel,
        (shape(RANK, COLS), shape(RANK, COLS), shape(COLS, COLS)),
        1 << 28,
        1 << 22,
        [pltpu.VMEM((COLS, COLS), F32)],
    )(tiles, slab, merged, right_init.T)
    return (left.T, right.T, new_memory[None])


def solution(mesh):
    return jax.shard_map(
        on_device,
        mesh=mesh,
        in_specs=(P("dp", "tensor"), P(("dp", "tensor"), None), P("dp", "tensor", None), P()),
        out_specs=(P("tensor", None), P(), P("dp", "tensor", None)),
        check_vma=False,
    )
```

time: 1040 us -> 207 us (0.20)
  waiting for transfers between devices: 867 us -> 52.4 us
  other arithmetic: 37.6 us -> 0 us
  Pallas kernels: 0 us -> 23.5 us
  matrix products: 21.6 us -> 3.51 us
  blocking collectives: 96.5 us -> 113 us
    psum x4 -> x0, waiting for transfers between devices: 814 us -> none  [the longest x2 526 us: on_device(): right = lax.psum(partial_right, ('dp', 'tensor')) / replicas]
    all_to_all x0 -> x4, blocking collectives: none -> 113 us  [exchange(): return lax.all_to_all(pieces, axis, 0, 0, tiled=False)]
    psum x2 -> x0, blocking collectives: 96.5 us -> none  [normalize(): gram = lax.psum(local_gram(left_raw), 'tensor')]
    another operation x10 -> x0, other arithmetic: 33.9 us -> none  [the longest x6 17.3 us: normalize(): lower = jnp.linalg.cholesky(gram)]
    pallas_call x0 -> x4, Pallas kernels: none -> 23.5 us  [the longest x1 21.8 us: on_device(): call(final_kernel, (shape(RANK, COLS), shape(RANK, COLS), shape(COLS, COL...]
    dot_general x7 -> x0, matrix products: 15 us -> none  [the longest x2 5.4 us: on_device(): local_left = jnp.dot(merged, right, precision=lax.Precision.HIGHEST)]
  transfers between devices with their start and end apart: 5 -> 1, of which waited for: 5 -> 1; matrix products, arithmetic and copies ran while one was open for 0% -> 0% of each run, Pallas kernels for 0% -> 0%
where the time goes in v2:
time: 207 us; the launch traced here: 206 us
  blocking collectives  113 us (55%)
  waiting for transfers between devices  52.4 us (25%)
  Pallas kernels  23.5 us (11%)
  between operations  14.1 us (7%)
  matrix products  3.51 us (2%)
    all_to_all x4, blocking collectives, exchange(): return lax.all_to_all(pieces, axis, 0, 0, tiled=False)  113 us
    all_gather x1, waiting for transfers between devices, on_device(): lax.all_gather(out_grad, 'tensor', axis=0, tiled=True)  51.7 us
    pallas_call x1, Pallas kernels, on_device(): call(final_kernel, (shape(RANK, COLS), shape(RANK, COLS), shape(COLS, COL...  21.8 us
  transfers between devices with their start and end apart: 1, of which 1 were waited for; matrix products, arithmetic and copies ran while one was open for 0% of the time, Pallas kernels for 0%

profile of v2, /device:TPU:1, one launch (start us, length us, event | category | flops | bytes accessed | tf_op | source)
XLA Modules:
  0.0 206.1 jit_solution(722254097215086485)
XLA Ops:
  7.2 0.0 copy-start
  7.2 0.0 all-gather.2.cloned.1.call-start
  7.2 0.7 all-gather.2.cloned.1.call-update
  7.9 51.7 %all-gather.2.cloned.1.call-done = bf16[2432,512]{1,0:T(8,128)(2,1)} async-done(((bf16[152,512]{1,0:T(8,128)(2,1)}), bf16[2432,512]{1,0:T(8,128)(2,1)}) %all-gather.2.cloned.1.call-update) | async-done | bytes 2490384 | tf_op jit(solution)/shard_map/all_gather | solution.py:112
  59.6 0.0 copy-done
  59.6 3.5 %convolution_add_fusion.merged_ref = f32[512,512]{1,0:T(8,128)S(1)} fusion(bf16[2432,512]{1,0:T(8,128)(2,1)S(1)} %copy-done, bf16[2432,512]{1,0:T(8,128)(2,1)} %all-gather.2.cloned.1.call-done, f32[1,512,512]{2,1,0:T(8,128)} %param.6), kind=kOutput, calls=%fused_computation | convolution fusion | flops 1275330560 | bytes 7077888 | tf_op jit(solution)/shard_map/dot_general | solution.py:110
  63.1 34.2 %all_to_all.20.parts_ref = f32[32,16,512]{2,1,0:T(8,128)S(1)} all-to-all(f32[32,16,512]{2,1,0:T(8,128)S(1)} %bitcast.13), channel_id=1, replica_groups=mesh['dp'=32,'tensor'=16] {'dp'}, dimensions={0} | all-to-all | bytes 2097152 | tf_op jit(solution)/shard_map/all_to_all | solution.py:26
  97.4 0.1 shard_map.67
  97.5 32.7 %all_to_all.21 = f32[32,16,512]{2,1,0:T(8,128)S(1)} all-to-all(f32[32,16,512]{2,1,0:T(8,128)S(1)} %shard_map.67), channel_id=1, replica_groups=mesh['dp'=32,'tensor'=16] {'dp'}, dimensions={0} | all-to-all | bytes 2097152 | tf_op jit(solution)/shard_map/all_to_all | solution.py:26
  130.2 0.0 copy-start.1
  130.2 1.5 shard_map.68
  131.7 22.0 %all_to_all.22.parts_ref = f32[16,8,640]{2,1,0:T(8,128)S(1)} all-to-all(f32[16,8,640]{2,1,0:T(8,128)S(1)} %shard_map.68), channel_id=1, replica_groups=mesh['dp'=32,'tensor'=16] {'tensor'}, dimensions={0} | all-to-all | bytes 655360 | tf_op jit(solution)/shard_map/all_to_all | solution.py:26
  153.7 0.1 shard_map.69
  153.8 23.6 %all_to_all.23 = f32[32,8,640]{2,1,0:T(8,128)S(1)} all-to-all(f32[32,8,640]{2,1,0:T(8,128)S(1)} %shard_map.69), channel_id=1, replica_groups=mesh['dp'=32,'tensor'=16] {'dp'}, dimensions={0} | all-to-all | bytes 1310720 | tf_op jit(solution)/shard_map/all_to_all | solution.py:26
  177.4 0.0 copy-done.1
  177.4 21.8 %shard_map.70 = (f32[64,512]{1,0:T(8,128)}, f32[64,512]{1,0:T(8,128)}, f32[512,512]{1,0:T(8,128)}) custom-call(f32[16,2,8,640]{3,2,1,0:T(8,128)S(1)} %bitcast.14, f32[512,512]{1,0:T(8,128)S(1)} %bitcast.12, f32[512,512]{1,0:T(8,128)S(1)} %convolution_add_fusion.merged_ref, f32[64,512]{1,0:T(8,128)S(1)} %bitcast.15), custom_call_target="tpu_custom_call" | custom-call | flops 268435456 | bytes 4194304 | tf_op jit(solution)/shard_map/pallas_call | solution.py:122
Async XLA Ops:
  7.2 52.4 %copy-start = (bf16[2432,512]{1,0:T(8,128)(2,1)S(1)}, bf16[2432,512]{1,0:T(8,128)(2,1)}, u32[]{:S(2)}) copy-start(bf16[2432,512]{1,0:T(8,128)(2,1)} %param.4) | copy-start | bytes 7471108
  7.2 52.4 %all-gather.2.cloned.1.call-start = ((), (), s32[]{:S(2)}) async-start(), calls=%async_computation.4 | async-start | bytes 2646016 | tf_op jit(solution)/shard_map/all_gather | solution.py:112
  130.2 47.1 %copy-start.1 = (f32[512,64]{0,1:T(8,128)S(1)}, f32[512,64]{0,1:T(8,128)}, u32[]{:S(2)}) copy-start(f32[512,64]{0,1:T(8,128)} %param.7) | copy-start | bytes 393220
Sparse Core Ops, SparseCore 0:
  10.1 49.4 all-gather.1

commit v3 on v2

--- a/solution.py
+++ b/solution.py
@@ -1,3 +1,4 @@
+import functools
 import math
 
 import jax
@@ -5,9 +6,9 @@
 from jax import lax
 from jax.experimental import pallas as pl
 from jax.experimental.pallas import tpu as pltpu
-from jax.sharding import PartitionSpec as P
+from jax.sharding import Mesh, PartitionSpec as P
 
-ROWS, COLS, RANK = 8192, 512, 64
+ROWS, COLS, RANK, TOKENS = 8192, 512, 64, 152
 F32 = jnp.float32
 PARAMS = pltpu.CompilerParams(vmem_limit_bytes=32 * 1024 * 1024)
 
@@ -24,6 +25,17 @@
 
 def exchange(pieces, axis):
     return lax.all_to_all(pieces, axis, 0, 0, tiled=False)
+
+
+def gradient_kernel(flip, tokens_ref, grads_ref, start_ref, out_ref):
+    core = lax.axis_index("core")
+    side = 1 - core if flip else core
+    total = start_ref[...]
+    for layer in range(tokens_ref.shape[0]):
+        total += lax.dot_general(
+            tokens_ref[layer, side], grads_ref[layer], (((0,), (0,)), ((), ())), preferred_element_type=F32
+        )
+    out_ref[...] = total
 
 
 def mean_kernel(parts_ref, copies_ref):
@@ -106,18 +118,20 @@
 
 
 def on_device(tokens_in, out_grad, memory, right_init):
-    replicas, pieces = lax.axis_size("dp"), lax.axis_size("tensor")
-    merged = memory[0] + lax.dot_general(
-        tokens_in,
-        lax.all_gather(out_grad, "tensor", axis=0, tiled=True),
-        (((0,), (0,)), ((), ())),
-        preferred_element_type=F32,
-    )
+    replicas, layers = lax.axis_size("dp"), lax.axis_size("z")
+    pieces = 2 * layers
+    tokens = tokens_in.reshape(layers, 2, TOKENS, COLS)
+    own = exchange(jnp.broadcast_to(out_grad[None], (layers, TOKENS, COLS)), "z")
+    other = lax.ppermute(own, "core", [(0, 1), (1, 0)])
+    half = call(functools.partial(gradient_kernel, 0), shape(COLS, COLS), 1 << 29, 1 << 22)
+    merged = half(tokens, own, memory[0])
+    half = call(functools.partial(gradient_kernel, 1), shape(COLS, COLS), 1 << 29, 1 << 22)
+    merged = half(tokens, other, merged)
     parts = exchange(merged.reshape(replicas, -1, COLS), "dp")
     copies = call(mean_kernel, shape(32, 16, COLS), 1 << 18, 1 << 21)(parts)
     slab = exchange(copies, "dp").reshape(COLS, COLS)
     copies = call(moment_kernel, shape(pieces, 8, 640), 1 << 26, 1 << 20)(slab)
-    copies = call(sum_kernel, shape(replicas, 8, 640), 1 << 17, 1 << 20)(exchange(copies, "tensor"))
+    copies = call(sum_kernel, shape(replicas, 8, 640), 1 << 17, 1 << 20)(exchange(copies, ("z", "core")))
     tiles = exchange(copies, "dp").reshape(16, 2, 8, 640)
     left, right, new_memory = call(
         final_kernel,
@@ -130,10 +144,13 @@
 
 
 def solution(mesh):
+    replicas, pieces = mesh.devices.shape
+    split = Mesh(mesh.devices.reshape(replicas, pieces // 2, 2), ("dp", "z", "core"))
+    tensor = ("z", "core")
     return jax.shard_map(
         on_device,
-        mesh=mesh,
-        in_specs=(P("dp", "tensor"), P(("dp", "tensor"), None), P("dp", "tensor", None), P()),
-        out_specs=(P("tensor", None), P(), P("dp", "tensor", None)),
+        mesh=split,
+        in_specs=(P("dp", tensor), P(("dp", "z", "core"), None), P("dp", tensor, None), P()),
+        out_specs=(P(tensor, None), P(), P("dp", tensor, None)),
         check_vma=False,
     )

time: 207 us -> 188 us (0.908)
  waiting for transfers between devices: 52.4 us -> 1.22 us
  blocking collectives: 113 us -> 153 us
  between operations: 14.1 us -> 0.71 us
  starting transfers between devices: 0.04 us -> 4.43 us
  matrix products: 3.51 us -> 0 us
  Pallas kernels: 23.5 us -> 26.1 us
    all_gather x1 -> x0, waiting for transfers between devices: 51.7 us -> none  [on_device(): lax.all_gather(out_grad, 'tensor', axis=0, tiled=True)]
    all_to_all x4 -> x5, blocking collectives: 113 us -> 153 us  [exchange(): return lax.all_to_all(pieces, axis, 0, 0, tiled=False)]
    ppermute x0 -> x1, starting transfers between devices: none -> 4.43 us  [on_device(): other = lax.ppermute(own, 'core', [(0, 1), (1, 0)])]
    dot_general x1 -> x0, matrix products: 3.51 us -> none  [on_device(): lax.dot_general(tokens_in, lax.all_gather(out_grad, 'tensor', axis=0, til...]
    pallas_call x0 -> x2, Pallas kernels: none -> 2.6 us  [the longest x1 1.3 us: on_device(): merged = half(tokens, other, merged)]
  transfers between devices with their start and end apart: 1 -> 1, of which waited for: 1 -> 1; matrix products, arithmetic and copies ran while one was open for 0% -> 0% of each run, Pallas kernels for 0% -> 1%
where the time goes in v3:
time: 188 us; the launch traced here: 187 us
  blocking collectives  153 us (81%)
  Pallas kernels  26.1 us (14%)
  starting transfers between devices  4.43 us (2%)
    all_to_all x5, blocking collectives, exchange(): return lax.all_to_all(pieces, axis, 0, 0, tiled=False)  153 us
    pallas_call x1, Pallas kernels, on_device(): call(final_kernel, (shape(RANK, COLS), shape(RANK, COLS), shape(COLS, COL...  21.8 us
    ppermute x1, starting transfers between devices, on_device(): other = lax.ppermute(own, 'core', [(0, 1), (1, 0)])  4.43 us
  transfers between devices with their start and end apart: 1, of which 1 were waited for; matrix products, arithmetic and copies ran while one was open for 0% of the time, Pallas kernels for 1%

profile of v3, /device:TPU:1, one launch (start us, length us, event | category | flops | bytes accessed | tf_op | source)
XLA Modules:
  0.0 187.0 jit_solution(14050042984495320968)
XLA Ops:
  0.6 0.0 copy-start.1
  0.6 1.1 broadcast_in_dim.4
  1.7 0.0 copy-start
  1.7 42.2 %all_to_all.25.grads_ref = bf16[8,152,512]{2,1,0:T(8,128)(2,1)S(1)} all-to-all(bf16[8,152,512]{2,1,0:T(8,128)(2,1)S(1)} %broadcast_in_dim.4), channel_id=1, replica_groups=mesh['dp'=32,'z'=8,'core'=2] {'z'}, dimensions={0} | all-to-all | bytes 2490368 | tf_op jit(solution)/shard_map/all_to_all | solution.py:27
  43.9 4.4 %collective-permute-start = (bf16[8,152,512]{2,1,0:T(8,128)(2,1)S(1)}, bf16[8,152,512]{2,1,0:T(8,128)(2,1)S(1)}, u32[]{:S(2)}, u32[]{:S(2)}) collective-permute-start(bf16[8,152,512]{2,1,0:T(8,128)(2,1)S(1)} %all_to_all.25.grads_ref), channel_id=1, source_target_pairs={{0,1},{1,0},{2,3},{3,2},{4,5},{5,4},{6,7},{7,6},{8,9},{9,8},{10,11... | collective-permute-start | bytes 3735560 | tf_op jit(solution)/shard_map/ppermute | solution.py:125
  48.3 0.0 copy-done.1
  48.3 0.0 copy-done
  48.4 1.3 shard_map.67.start_ref
  49.7 1.2 collective-permute-done.grads_ref
  50.9 1.3 shard_map.68.merged_ref
  52.2 34.7 %all_to_all.26.parts_ref = f32[32,16,512]{2,1,0:T(8,128)S(1)} all-to-all(f32[32,16,512]{2,1,0:T(8,128)S(1)} %bitcast.13), channel_id=1, replica_groups=mesh['dp'=32,'z'=8,'core'=2] {'dp'}, dimensions={0} | all-to-all | bytes 2097152 | tf_op jit(solution)/shard_map/all_to_all | solution.py:27
  86.9 0.1 shard_map.69
  87.0 32.4 %all_to_all.27 = f32[32,16,512]{2,1,0:T(8,128)S(1)} all-to-all(f32[32,16,512]{2,1,0:T(8,128)S(1)} %shard_map.69), channel_id=1, replica_groups=mesh['dp'=32,'z'=8,'core'=2] {'dp'}, dimensions={0} | all-to-all | bytes 2097152 | tf_op jit(solution)/shard_map/all_to_all | solution.py:27
  119.4 1.5 shard_map.70
  120.9 20.6 %all_to_all.28.parts_ref = f32[16,8,640]{2,1,0:T(8,128)S(1)} all-to-all(f32[16,8,640]{2,1,0:T(8,128)S(1)} %shard_map.70), channel_id=1, replica_groups=mesh['dp'=32,'z'=8,'core'=2] {'z','core'}, dimensions={0} | all-to-all | bytes 655360 | tf_op jit(solution)/shard_map/all_to_all | solution.py:27
  141.5 0.0 copy-start.2
  141.5 0.1 shard_map.71
  141.5 23.6 %all_to_all.29 = f32[32,8,640]{2,1,0:T(8,128)S(1)} all-to-all(f32[32,8,640]{2,1,0:T(8,128)S(1)} %shard_map.71), channel_id=1, replica_groups=mesh['dp'=32,'z'=8,'core'=2] {'dp'}, dimensions={0} | all-to-all | bytes 1310720 | tf_op jit(solution)/shard_map/all_to_all | solution.py:27
  165.1 0.0 copy-done.2
  165.1 21.8 %shard_map.72 = (f32[64,512]{1,0:T(8,128)}, f32[64,512]{1,0:T(8,128)}, f32[512,512]{1,0:T(8,128)}) custom-call(f32[16,2,8,640]{3,2,1,0:T(8,128)S(1)} %bitcast.14, f32[512,512]{1,0:T(8,128)S(1)} %bitcast.12, f32[512,512]{1,0:T(8,128)S(1)} %shard_map.68.merged_ref, f32[64,512]{1,0:T(8,128)S(1)} %bitcast.16), custom_call_target="tpu_custom_call" | custom-call | flops 268435456 | bytes 4194304 | tf_op jit(solution)/shard_map/pallas_call | solution.py:136
Async XLA Ops:
  0.6 47.7 %copy-start.1 = (f32[1,512,512]{2,1,0:T(8,128)S(1)}, f32[1,512,512]{2,1,0:T(8,128)}, u32[]{:S(2)}) copy-start(f32[1,512,512]{2,1,0:T(8,128)} %param.6) | copy-start | bytes 3145732
  1.7 46.6 %copy-start = (bf16[2432,512]{1,0:T(8,128)(2,1)S(1)}, bf16[2432,512]{1,0:T(8,128)(2,1)}, u32[]{:S(2)}) copy-start(bf16[2432,512]{1,0:T(8,128)(2,1)} %param.4) | copy-start | bytes 7471108
  43.9 7.0 %collective-permute-start = (bf16[8,152,512]{2,1,0:T(8,128)(2,1)S(1)}, bf16[8,152,512]{2,1,0:T(8,128)(2,1)S(1)}, u32[]{:S(2)}, u32[]{:S(2)}) collective-permute-start(bf16[8,152,512]{2,1,0:T(8,128)(2,1)S(1)} %all_to_all.25.grads_ref), channel_id=1, source_target_pairs={{0,1},{1,0},{2,3},{3,2},{4,5},{5,4},{6,7},{7,6},{8,9},{9,8},{10,11... | collective-permute-start | bytes 3735560 | tf_op jit(solution)/shard_map/ppermute | solution.py:125
  141.5 23.6 %copy-start.2 = (f32[512,64]{0,1:T(8,128)S(1)}, f32[512,64]{0,1:T(8,128)}, u32[]{:S(2)}) copy-start(f32[512,64]{0,1:T(8,128)} %param.7) | copy-start | bytes 393220

commit v4 on v3

--- a/solution.py
+++ b/solution.py
@@ -46,19 +46,20 @@
 
 def moment_kernel(slab_ref, copies_ref):
     position = lax.axis_index("dp")
-    offset = 8 * lax.div(position, 2)
-    odd = lax.rem(position, 2) == 1
-    first = jnp.where(odd, 128, 0) + offset
-    second = jnp.where(odd, 256, 384) + offset - 8
+    high = lax.rem(position, 2) == 1
+    first = jnp.where(high, 256, 0) + 8 * lax.div(position, 2)
     step = lax.broadcasted_iota(jnp.int32, (16, COLS), 0)
-    wanted = step + jnp.where(step < 8, first, second)
+    wanted = step + jnp.where(step < 8, first, first + 120)
     pick = jnp.where(lax.broadcasted_iota(jnp.int32, (16, COLS), 1) == wanted, 1.0, 0.0)
     slab = slab_ref[...]
     rows = dot(dot(pick, slab, 1, 1), slab, 1, 0)
-    low = jnp.concatenate([rows[:8, :], rows[8:, 384:]], axis=1)
-    high = jnp.concatenate([rows[:8, 128:], rows[8:, 256:]], axis=1)
-    tiles = jnp.where(odd, high, low)
-    copies_ref[...] = jnp.broadcast_to(tiles[None], copies_ref.shape)
+    for core, row in enumerate((rows[:8], rows[8:])):
+        turned = jnp.concatenate([row, row], axis=1)
+        near = turned[:, 128 * core : 128 * core + 384]
+        far = turned[:, 128 * core + 256 : 128 * core + 640]
+        tiles = jnp.where(high, far, near)
+        for layer in range(copies_ref.shape[0] // 2):
+            copies_ref[2 * layer + core] = tiles
 
 
 def sum_kernel(parts_ref, copies_ref):
@@ -73,27 +74,46 @@
     for b in range(8):
         wide = jnp.concatenate([gram[8 * b : 8 * b + 8], jnp.zeros((8, RANK), F32)], axis=1)
         blocks.append(jnp.where(lane == RANK + 8 * b + row, 1.0, wide))
-    for k in range(RANK):
-        own, r = divmod(k, 8)
-        pivot_row = jnp.broadcast_to(blocks[own][r : r + 1], (8, 128))
-        scale = lax.rsqrt(jnp.broadcast_to(pivot_row[:, k : k + 1], (8, 128)))
-        scaled = pivot_row * scale
-        for b in range(own, 8):
-            new = blocks[b] - jnp.broadcast_to(blocks[b][:, k : k + 1], (8, 128)) * scale * scaled
-            if b == own:
-                new = jnp.where(row > r, new, jnp.where(row == r, scaled, blocks[b]))
-            blocks[b] = new
+
+    def spread(part):
+        return jnp.broadcast_to(part, (8, 128))
+
+    for p in range(8):
+        rows = [spread(blocks[p][i : i + 1]) for i in range(8)]
+        entry = {(i, j): spread(rows[i][:, 8 * p + j : 8 * p + j + 1]) for i in range(8) for j in range(i, 8)}
+        columns = {
+            b: [spread(blocks[b][:, 8 * p + j : 8 * p + j + 1]) for j in range(8)] for b in range(p + 1, 8)
+        }
+        for i in range(8):
+            scale = lax.rsqrt(entry[i, i])
+            rows[i] = rows[i] * scale
+            for column in columns.values():
+                column[i] = column[i] * scale
+            factor = {j: entry[i, j] * scale for j in range(i + 1, 8)}
+            for k in range(i + 1, 8):
+                for j in range(k, 8):
+                    entry[k, j] = entry[k, j] - factor[k] * factor[j]
+                rows[k] = rows[k] - factor[k] * rows[i]
+                for column in columns.values():
+                    column[k] = column[k] - factor[k] * column[i]
+        for b, column in columns.items():
+            for i in range(8):
+                blocks[b] = blocks[b] - column[i] * rows[i]
+        done = rows[0]
+        for i in range(1, 8):
+            done = jnp.where(row == i, rows[i], done)
+        blocks[p] = done
     return jnp.concatenate([block[:, RANK:] for block in blocks], axis=0)
 
 
 def final_kernel(tiles_ref, slab_ref, merged_ref, right_ref, left_out, right_out, memory_out, moment):
-    places = {(i, j): (i, j - i) for i in range(2) for j in range(i, 4)}
-    places |= {(2, 2): (1, 3), (2, 3): (1, 4), (3, 3): (0, 4)}
-    for (i, j), (h, t) in places.items():
-        block = tiles_ref[:, h, :, 128 * t : 128 * t + 128].reshape(128, 128)
-        moment[128 * i : 128 * i + 128, 128 * j : 128 * j + 128] = block
-        if i != j:
-            moment[128 * j : 128 * j + 128, 128 * i : 128 * i + 128] = block.T
+    for b in range(4):
+        for j in range(3):
+            block = tiles_ref[b % 2, :, b // 2, :, 128 * j : 128 * j + 128].reshape(128, 128)
+            to = (b + j) % 4
+            moment[128 * b : 128 * b + 128, 128 * to : 128 * to + 128] = block
+            if j == 1:
+                moment[128 * to : 128 * to + 128, 128 * b : 128 * b + 128] = block.T
     start = right_ref[...]
     image = dot(start, moment[...], 1, 0)
     right = dot(inverse_factor(dot(start, image, 1, 1)), image, 1, 0)
@@ -130,9 +150,9 @@
     parts = exchange(merged.reshape(replicas, -1, COLS), "dp")
     copies = call(mean_kernel, shape(32, 16, COLS), 1 << 18, 1 << 21)(parts)
     slab = exchange(copies, "dp").reshape(COLS, COLS)
-    copies = call(moment_kernel, shape(pieces, 8, 640), 1 << 26, 1 << 20)(slab)
-    copies = call(sum_kernel, shape(replicas, 8, 640), 1 << 17, 1 << 20)(exchange(copies, ("z", "core")))
-    tiles = exchange(copies, "dp").reshape(16, 2, 8, 640)
+    copies = call(moment_kernel, shape(pieces, 8, 384), 1 << 26, 1 << 20)(slab)
+    copies = call(sum_kernel, shape(replicas, 8, 384), 1 << 17, 1 << 20)(exchange(copies, ("z", "core")))
+    tiles = lax.all_gather(exchange(copies, "dp"), "core").reshape(2, 16, 2, 8, 384)
     left, right, new_memory = call(
         final_kernel,
         (shape(RANK, COLS), shape(RANK, COLS), shape(COLS, COLS)),

time: 188 us -> 170 us (0.904)
  Pallas kernels: 26.1 us -> 13.1 us
  blocking collectives: 153 us -> 149 us
    pallas_call x1, Pallas kernels: 21.8 us -> 8.83 us  [on_device(): call(final_kernel, (shape(RANK, COLS), shape(RANK, COLS), shape(COLS, COL...]
    all_to_all x5, blocking collectives: 153 us -> 145 us  [exchange(): return lax.all_to_all(pieces, axis, 0, 0, tiled=False)]
    all_gather x0 -> x1, blocking collectives: none -> 3.93 us  [on_device(): lax.all_gather(exchange(copies, 'dp'), 'core').reshape(2, 16, 2, 8, 384)]
where the time goes in v4:
time: 170 us; the launch traced here: 169 us
  blocking collectives  149 us (88%)
  Pallas kernels  13.1 us (8%)
  starting transfers between devices  4.43 us (3%)
    all_to_all x5, blocking collectives, exchange(): return lax.all_to_all(pieces, axis, 0, 0, tiled=False)  145 us
    pallas_call x1, Pallas kernels, on_device(): call(final_kernel, (shape(RANK, COLS), shape(RANK, COLS), shape(COLS, COL...  8.83 us
    ppermute x1, starting transfers between devices, on_device(): other = lax.ppermute(own, 'core', [(0, 1), (1, 0)])  4.43 us
    all_gather x1, blocking collectives, on_device(): lax.all_gather(exchange(copies, 'dp'), 'core').reshape(2, 16, 2, 8, 384)  3.93 us
  transfers between devices with their start and end apart: 1, of which 1 were waited for; matrix products, arithmetic and copies ran while one was open for 0% of the time, Pallas kernels for 1%

profile of v4, /device:TPU:1, one launch (start us, length us, event | category | flops | bytes accessed | tf_op | source)
XLA Modules:
  0.0 169.4 jit_solution(10743375469757061476)
XLA Ops:
  0.6 0.0 copy-start.1
  0.6 1.1 broadcast_in_dim.4
  1.7 0.0 copy-start
  1.7 42.2 %all_to_all.25.grads_ref = bf16[8,152,512]{2,1,0:T(8,128)(2,1)S(1)} all-to-all(bf16[8,152,512]{2,1,0:T(8,128)(2,1)S(1)} %broadcast_in_dim.4), channel_id=1, replica_groups=mesh['dp'=32,'z'=8,'core'=2] {'z'}, dimensions={0} | all-to-all | bytes 2490368 | tf_op jit(solution)/shard_map/all_to_all | solution.py:27
  43.9 4.4 %collective-permute-start = (bf16[8,152,512]{2,1,0:T(8,128)(2,1)S(1)}, bf16[8,152,512]{2,1,0:T(8,128)(2,1)S(1)}, u32[]{:S(2)}, u32[]{:S(2)}) collective-permute-start(bf16[8,152,512]{2,1,0:T(8,128)(2,1)S(1)} %all_to_all.25.grads_ref), channel_id=1, source_target_pairs={{0,1},{1,0},{2,3},{3,2},{4,5},{5,4},{6,7},{7,6},{8,9},{9,8},{10,11... | collective-permute-start | bytes 3735560 | tf_op jit(solution)/shard_map/ppermute | solution.py:145
  48.3 0.0 copy-done.1
  48.3 0.0 copy-done
  48.4 1.3 shard_map.67.start_ref
  49.7 1.2 collective-permute-done.grads_ref
  50.9 1.3 shard_map.68.merged_ref
  52.2 34.7 %all_to_all.26.parts_ref = f32[32,16,512]{2,1,0:T(8,128)S(1)} all-to-all(f32[32,16,512]{2,1,0:T(8,128)S(1)} %bitcast.13), channel_id=1, replica_groups=mesh['dp'=32,'z'=8,'core'=2] {'dp'}, dimensions={0} | all-to-all | bytes 2097152 | tf_op jit(solution)/shard_map/all_to_all | solution.py:27
  86.9 0.1 shard_map.69
  87.0 32.4 %all_to_all.27 = f32[32,16,512]{2,1,0:T(8,128)S(1)} all-to-all(f32[32,16,512]{2,1,0:T(8,128)S(1)} %shard_map.69), channel_id=1, replica_groups=mesh['dp'=32,'z'=8,'core'=2] {'dp'}, dimensions={0} | all-to-all | bytes 2097152 | tf_op jit(solution)/shard_map/all_to_all | solution.py:27
  119.4 1.5 shard_map.70
  120.9 17.9 %all_to_all.28.parts_ref = f32[16,8,384]{2,1,0:T(8,128)S(1)} all-to-all(f32[16,8,384]{2,1,0:T(8,128)S(1)} %shard_map.70), channel_id=1, replica_groups=mesh['dp'=32,'z'=8,'core'=2] {'z','core'}, dimensions={0} | all-to-all | bytes 393216 | tf_op jit(solution)/shard_map/all_to_all | solution.py:27
  138.8 0.0 copy-start.2
  138.8 17.8 %all_to_all.29 = f32[32,8,384]{2,1,0:T(8,128)S(1)} all-to-all(f32[32,8,384]{2,1,0:T(8,128)S(1)} %shard_map.71), channel_id=1, replica_groups=mesh['dp'=32,'z'=8,'core'=2] {'dp'}, dimensions={0} | all-to-all | bytes 786432 | tf_op jit(solution)/shard_map/all_to_all | solution.py:27
  156.6 3.9 %all-gather = f32[64,8,384]{2,1,0:T(8,128)S(1)} all-gather(f32[32,8,384]{2,1,0:T(8,128)S(1)} %all_to_all.29), channel_id=2, replica_groups=mesh['dp'=32,'z'=8,'core'=2] {'core'}, dimensions={0}, use_global_device_ids=true | all-gather | bytes 1179648 | tf_op jit(solution)/shard_map/all_gather | solution.py:155
  160.6 0.0 copy-done.2
  160.6 8.8 %shard_map.72 = (f32[64,512]{1,0:T(8,128)}, f32[64,512]{1,0:T(8,128)}, f32[512,512]{1,0:T(8,128)}) custom-call(f32[2,16,2,8,384]{4,3,2,1,0:T(8,128)S(1)} %bitcast.14, f32[512,512]{1,0:T(8,128)S(1)} %bitcast.12, f32[512,512]{1,0:T(8,128)S(1)} %shard_map.68.merged_ref, f32[64,512]{1,0:T(8,128)S(1)} %bitcast.16), custom_call_target="tpu_custom_call" | custom-call | flops 268435456 | bytes 4194304 | tf_op jit(solution)/shard_map/pallas_call | solution.py:156
  (1 shorter events, 0.0 us)
Async XLA Ops:
  0.6 47.7 %copy-start.1 = (f32[1,512,512]{2,1,0:T(8,128)S(1)}, f32[1,512,512]{2,1,0:T(8,128)}, u32[]{:S(2)}) copy-start(f32[1,512,512]{2,1,0:T(8,128)} %param.6) | copy-start | bytes 3145732
  1.7 46.6 %copy-start = (bf16[2432,512]{1,0:T(8,128)(2,1)S(1)}, bf16[2432,512]{1,0:T(8,128)(2,1)}, u32[]{:S(2)}) copy-start(bf16[2432,512]{1,0:T(8,128)(2,1)} %param.4) | copy-start | bytes 7471108
  43.9 7.0 %collective-permute-start = (bf16[8,152,512]{2,1,0:T(8,128)(2,1)S(1)}, bf16[8,152,512]{2,1,0:T(8,128)(2,1)S(1)}, u32[]{:S(2)}, u32[]{:S(2)}) collective-permute-start(bf16[8,152,512]{2,1,0:T(8,128)(2,1)S(1)} %all_to_all.25.grads_ref), channel_id=1, source_target_pairs={{0,1},{1,0},{2,3},{3,2},{4,5},{5,4},{6,7},{7,6},{8,9},{9,8},{10,11... | collective-permute-start | bytes 3735560 | tf_op jit(solution)/shard_map/ppermute | solution.py:145
  138.8 21.8 %copy-start.2 = (f32[512,64]{0,1:T(8,128)S(1)}, f32[512,64]{0,1:T(8,128)}, u32[]{:S(2)}) copy-start(f32[512,64]{0,1:T(8,128)} %param.7) | copy-start | bytes 393220

commit v5 on v4

--- a/solution.py
+++ b/solution.py
@@ -10,6 +10,7 @@
 
 ROWS, COLS, RANK, TOKENS = 8192, 512, 64, 152
 F32 = jnp.float32
+SPLIT = 384
 PARAMS = pltpu.CompilerParams(vmem_limit_bytes=32 * 1024 * 1024)
 
 
@@ -27,7 +28,14 @@
     return lax.all_to_all(pieces, axis, 0, 0, tiled=False)
 
 
-def gradient_kernel(flip, tokens_ref, grads_ref, start_ref, out_ref):
+def product_kernel(tokens_ref, grads_ref, start_ref, out_ref):
+    out_ref[...] = start_ref[...] + lax.dot_general(
+        tokens_ref[...], grads_ref[...], (((0,), (0,)), ((), ())), preferred_element_type=F32
+    )
+
+
+def gradient_kernel(flip, tokens_ref, grads_ref, start_ref, *refs):
+    *tail_refs, out_ref = refs
     core = lax.axis_index("core")
     side = 1 - core if flip else core
     total = start_ref[...]
@@ -35,7 +43,9 @@
         total += lax.dot_general(
             tokens_ref[layer, side], grads_ref[layer], (((0,), (0,)), ((), ())), preferred_element_type=F32
         )
-    out_ref[...] = total
+    out_ref[:, :SPLIT] = total
+    for tail_ref in tail_refs:
+        out_ref[:, SPLIT:] = tail_ref[...]
 
 
 def mean_kernel(parts_ref, copies_ref):
@@ -141,12 +151,15 @@
     replicas, layers = lax.axis_size("dp"), lax.axis_size("z")
     pieces = 2 * layers
     tokens = tokens_in.reshape(layers, 2, TOKENS, COLS)
-    own = exchange(jnp.broadcast_to(out_grad[None], (layers, TOKENS, COLS)), "z")
+    own = exchange(jnp.broadcast_to(out_grad[None, :, :SPLIT], (layers, TOKENS, SPLIT)), "z")
+    grads = lax.all_gather(out_grad[:, SPLIT:], ("z", "core"), axis=0, tiled=True)
+    tail = call(product_kernel, shape(COLS, COLS - SPLIT), 1 << 28, 1 << 22)(tokens_in, grads, memory[0, :, SPLIT:])
+    own, tail = lax.optimization_barrier((own, tail))
     other = lax.ppermute(own, "core", [(0, 1), (1, 0)])
-    half = call(functools.partial(gradient_kernel, 0), shape(COLS, COLS), 1 << 29, 1 << 22)
-    merged = half(tokens, own, memory[0])
-    half = call(functools.partial(gradient_kernel, 1), shape(COLS, COLS), 1 << 29, 1 << 22)
-    merged = half(tokens, other, merged)
+    half = call(functools.partial(gradient_kernel, 0), shape(COLS, SPLIT), 1 << 29, 1 << 22)
+    merged = half(tokens, own, memory[0, :, :SPLIT])
+    whole = call(functools.partial(gradient_kernel, 1), shape(COLS, COLS), 1 << 29, 1 << 22)
+    merged = whole(tokens, other, merged, tail)
     parts = exchange(merged.reshape(replicas, -1, COLS), "dp")
     copies = call(mean_kernel, shape(32, 16, COLS), 1 << 18, 1 << 21)(parts)
     slab = exchange(copies, "dp").reshape(COLS, COLS)

time: 170 us -> 178 us (1.047)
  starting transfers between devices: 4.43 us -> 12.9 us
  blocking collectives: 149 us -> 145 us
  local copies, waits for them, and re-layouts: 1.1 us -> 4.93 us
    all_to_all x5 -> x4, blocking collectives: 145 us -> 105 us  [exchange(): return lax.all_to_all(pieces, axis, 0, 0, tiled=False)]
    all_gather x0 -> x1, blocking collectives: none -> 35.9 us  [on_device(): lax.all_gather(out_grad[:, SPLIT:], ('z', 'core'), axis=0, tiled=True)]
    all_to_all x0 -> x1, starting transfers between devices: none -> 10.9 us  [exchange(): return lax.all_to_all(pieces, axis, 0, 0, tiled=False)]
    ppermute x1, starting transfers between devices: 4.43 us -> 2.06 us  [on_device(): other = lax.ppermute(own, 'core', [(0, 1), (1, 0)])]
    squeeze x0 -> x2, local copies, waits for them, and re-layouts: none -> 2.15 us  [the longest x1 1.19 us: on_device(): merged = half(tokens, own, memory[0, :, :SPLIT])]
  transfers between devices with their start and end apart: 1 -> 2, of which waited for: 1 -> 0; matrix products, arithmetic and copies ran while one was open for 0% -> 1% of each run, Pallas kernels for 1% -> 1%
where the time goes in v5:
time: 178 us
  blocking collectives  145 us (81%)
  Pallas kernels  13.9 us (8%)
  starting transfers between devices  12.9 us (7%)
  local copies, waits for them, and re-layouts  4.93 us (3%)
    all_to_all x4, blocking collectives, exchange(): return lax.all_to_all(pieces, axis, 0, 0, tiled=False)  105 us
    all_gather x1, blocking collectives, on_device(): lax.all_gather(out_grad[:, SPLIT:], ('z', 'core'), axis=0, tiled=True)  35.9 us
    all_to_all x1, starting transfers between devices, exchange(): return lax.all_to_all(pieces, axis, 0, 0, tiled=False)  10.9 us
    pallas_call x1, Pallas kernels, on_device(): call(final_kernel, (shape(RANK, COLS), shape(RANK, COLS), shape(COLS, COL...  8.82 us
    all_gather x1, blocking collectives, on_device(): lax.all_gather(exchange(copies, 'dp'), 'core').reshape(2, 16, 2, 8, 384)  4.07 us
  transfers between devices with their start and end apart: 2, of which 0 were waited for; matrix products, arithmetic and copies ran while one was open for 1% of the time, Pallas kernels for 1%

profile of v5, /device:TPU:1, one launch (start us, length us, event | category | flops | bytes accessed | tf_op | source)
XLA Modules:
  0.0 177.9 jit_solution(5086366690683823463)
XLA Ops:
  0.6 0.0 slice-start
  0.6 0.0 copy-start
  0.7 1.1 slice.12
  1.7 1.0 broadcast_in_dim.4
  2.7 10.9 %all-to-all-start = ((bf16[8,152,384]{2,1,0:T(8,128)(2,1)}), bf16[8,152,384]{2,1,0:T(8,128)(2,1)S(1)}, u32[]{:S(2)}, u32[]{:S(2)}) async-start(bf16[8,152,384]{2,1,0:T(8,128)(2,1)} %broadcast_in_dim.4), calls=%async_computation | async-start | bytes 1867776 | tf_op jit(solution)/shard_map/all_to_all | solution.py:28
  13.6 1.0 slice_bitcast_fusion.1.start_ref
  14.6 0.0 slice-done
  14.6 35.9 %all_gather.9.grads_ref = bf16[2432,128]{1,0:T(8,128)(2,1)S(1)} all-gather(bf16[152,128]{1,0:T(8,128)(2,1)S(1)} %slice-done), channel_id=1, replica_groups=mesh['dp'=32,'z'=8,'core'=2] {'z','core'}, dimensions={0}, use_global_device_ids=true | all-gather | bytes 661504 | tf_op jit(solution)/shard_map/all_gather | solution.py:155
  50.5 0.9 shard_map.67.refs_0_
  51.3 0.7 copy-done.1
  52.0 0.0 all-to-all-done.grads_ref
  52.0 2.1 %collective-permute-start = (bf16[8,152,384]{2,1,0:T(8,128)(2,1)S(1)}, bf16[8,152,384]{2,1,0:T(8,128)(2,1)S(1)}, u32[]{:S(2)}, u32[]{:S(2)}) collective-permute-start(bf16[8,152,384]{2,1,0:T(8,128)(2,1)S(1)} %all-to-all-done.grads_ref), channel_id=1, source_target_pairs={{0,1},{1,0},{2,3},{3,2},{4,5},{5,4},{6,7},{7,6},{8,9},{9,8},{10,11... | collective-permute-start | bytes 2801672 | tf_op jit(solution)/shard_map/ppermute | solution.py:158
  54.1 1.2 slice_bitcast_fusion.start_ref
  55.3 1.3 shard_map.68.start_ref
  56.6 0.0 collective-permute-done.grads_ref
  56.6 1.3 shard_map.69.merged_ref
  57.9 34.7 %all_to_all.25.parts_ref = f32[32,16,512]{2,1,0:T(8,128)S(1)} all-to-all(f32[32,16,512]{2,1,0:T(8,128)S(1)} %bitcast.16), channel_id=1, replica_groups=mesh['dp'=32,'z'=8,'core'=2] {'dp'}, dimensions={0} | all-to-all | bytes 2097152 | tf_op jit(solution)/shard_map/all_to_all | solution.py:28
  92.6 0.1 shard_map.70
  92.8 32.4 %all_to_all.26 = f32[32,16,512]{2,1,0:T(8,128)S(1)} all-to-all(f32[32,16,512]{2,1,0:T(8,128)S(1)} %shard_map.70), channel_id=1, replica_groups=mesh['dp'=32,'z'=8,'core'=2] {'dp'}, dimensions={0} | all-to-all | bytes 2097152 | tf_op jit(solution)/shard_map/all_to_all | solution.py:28
  125.2 1.5 shard_map.71
  126.7 20.7 %all_to_all.27.parts_ref = f32[16,8,384]{2,1,0:T(8,128)S(1)} all-to-all(f32[16,8,384]{2,1,0:T(8,128)S(1)} %shard_map.71), channel_id=1, replica_groups=mesh['dp'=32,'z'=8,'core'=2] {'z','core'}, dimensions={0} | all-to-all | bytes 393216 | tf_op jit(solution)/shard_map/all_to_all | solution.py:28
  147.5 17.6 %all_to_all.28 = f32[32,8,384]{2,1,0:T(8,128)S(1)} all-to-all(f32[32,8,384]{2,1,0:T(8,128)S(1)} %shard_map.72), channel_id=1, replica_groups=mesh['dp'=32,'z'=8,'core'=2] {'dp'}, dimensions={0} | all-to-all | bytes 786432 | tf_op jit(solution)/shard_map/all_to_all | solution.py:28
  165.0 4.1 %all-gather = f32[64,8,384]{2,1,0:T(8,128)S(1)} all-gather(f32[32,8,384]{2,1,0:T(8,128)S(1)} %all_to_all.28), channel_id=2, replica_groups=mesh['dp'=32,'z'=8,'core'=2] {'core'}, dimensions={0}, use_global_device_ids=true | all-gather | bytes 1179648 | tf_op jit(solution)/shard_map/all_gather | solution.py:168
  169.1 8.8 %shard_map.73 = (f32[64,512]{1,0:T(8,128)}, f32[64,512]{1,0:T(8,128)}, f32[512,512]{1,0:T(8,128)}) custom-call(f32[2,16,2,8,384]{4,3,2,1,0:T(8,128)S(1)} %bitcast.17, f32[512,512]{1,0:T(8,128)S(1)} %bitcast.15, f32[512,512]{1,0:T(8,128)S(1)} %shard_map.69.merged_ref, f32[64,512]{1,0:T(8,128)S(1)} %bitcast.18), custom_call_target="tpu_custom_call" | custom-call | flops 268435456 | bytes 4194304 | tf_op jit(solution)/shard_map/pallas_call | solution.py:169
  (7 shorter events, 0.1 us)
Async XLA Ops:
  0.6 13.9 %slice-start = ((bf16[152,512]{1,0:T(8,128)(2,1)}), bf16[152,128]{1,0:T(8,128)(2,1)S(1)}, s32[]{:S(2)}) async-start(bf16[152,512]{1,0:T(8,128)(2,1)} %param.5), calls=%async_computation.5 | async-start | bytes 77824 | tf_op jit(solution)/shard_map/slice | solution.py:155
  0.6 49.8 %copy-start = (bf16[2432,512]{1,0:T(8,128)(2,1)S(1)}, bf16[2432,512]{1,0:T(8,128)(2,1)}, u32[]{:S(2)}) copy-start(bf16[2432,512]{1,0:T(8,128)(2,1)} %tokens_ref.1) | copy-start | bytes 7471108
  2.7 49.3 %all-to-all-start = ((bf16[8,152,384]{2,1,0:T(8,128)(2,1)}), bf16[8,152,384]{2,1,0:T(8,128)(2,1)S(1)}, u32[]{:S(2)}, u32[]{:S(2)}) async-start(bf16[8,152,384]{2,1,0:T(8,128)(2,1)} %broadcast_in_dim.4), calls=%async_computation | async-start | bytes 1867776 | tf_op jit(solution)/shard_map/all_to_all | solution.py:28
  51.3 0.7 copy-start.1
  52.0 4.6 %collective-permute-start = (bf16[8,152,384]{2,1,0:T(8,128)(2,1)S(1)}, bf16[8,152,384]{2,1,0:T(8,128)(2,1)S(1)}, u32[]{:S(2)}, u32[]{:S(2)}) collective-permute-start(bf16[8,152,384]{2,1,0:T(8,128)(2,1)S(1)} %all-to-all-done.grads_ref), channel_id=1, source_target_pairs={{0,1},{1,0},{2,3},{3,2},{4,5},{5,4},{6,7},{7,6},{8,9},{9,8},{10,11... | collective-permute-start | bytes 2801672 | tf_op jit(solution)/shard_map/ppermute | solution.py:158
  55.3 1.3 copy-start.2
  125.2 43.9 %copy-start.3 = (f32[512,64]{0,1:T(8,128)S(1)}, f32[512,64]{0,1:T(8,128)}, u32[]{:S(2)}) copy-start(f32[512,64]{0,1:T(8,128)} %param.7) | copy-start | bytes 393220

commit v6 on v4

--- a/solution.py
+++ b/solution.py
@@ -38,14 +38,17 @@
     out_ref[...] = total
 
 
-def mean_kernel(parts_ref, copies_ref):
-    count = parts_ref.shape[0]
+def partial_kernel(parts_ref, part_ref):
+    part_ref[...] = jnp.sum(parts_ref[...], axis=0)
+
+
+def mean_kernel(count, parts_ref, copies_ref):
     mean = jnp.sum(parts_ref[...], axis=0) * (1.0 / count)
     copies_ref[...] = jnp.broadcast_to(mean[None], copies_ref.shape)
 
 
 def moment_kernel(slab_ref, copies_ref):
-    position = lax.axis_index("dp")
+    position = lax.axis_index("x") * lax.axis_size("y") + lax.axis_index("y")
     high = lax.rem(position, 2) == 1
     first = jnp.where(high, 256, 0) + 8 * lax.div(position, 2)
     step = lax.broadcasted_iota(jnp.int32, (16, COLS), 0)
@@ -138,7 +141,8 @@
 
 
 def on_device(tokens_in, out_grad, memory, right_init):
-    replicas, layers = lax.axis_size("dp"), lax.axis_size("z")
+    replicas, layers = lax.axis_size(("x", "y")), lax.axis_size("z")
+    rows = lax.axis_size("x")
     pieces = 2 * layers
     tokens = tokens_in.reshape(layers, 2, TOKENS, COLS)
     own = exchange(jnp.broadcast_to(out_grad[None], (layers, TOKENS, COLS)), "z")
@@ -147,12 +151,16 @@
     merged = half(tokens, own, memory[0])
     half = call(functools.partial(gradient_kernel, 1), shape(COLS, COLS), 1 << 29, 1 << 22)
     merged = half(tokens, other, merged)
-    parts = exchange(merged.reshape(replicas, -1, COLS), "dp")
-    copies = call(mean_kernel, shape(32, 16, COLS), 1 << 18, 1 << 21)(parts)
-    slab = exchange(copies, "dp").reshape(COLS, COLS)
+    parts = exchange(merged.reshape(rows, -1, COLS), "x")
+    part = call(partial_kernel, shape(COLS // rows, COLS), 1 << 18, 1 << 20)(parts)
+    parts = exchange(part.reshape(replicas // rows, -1, COLS), "y")
+    scaled = functools.partial(mean_kernel, replicas)
+    copies = call(scaled, shape(replicas // rows, 16, COLS), 1 << 16, 1 << 20)(parts)
+    part = exchange(copies, "y").reshape(COLS // rows, COLS)
+    slab = exchange(jnp.broadcast_to(part[None], (rows,) + part.shape), "x").reshape(COLS, COLS)
     copies = call(moment_kernel, shape(pieces, 8, 384), 1 << 26, 1 << 20)(slab)
     copies = call(sum_kernel, shape(replicas, 8, 384), 1 << 17, 1 << 20)(exchange(copies, ("z", "core")))
-    tiles = lax.all_gather(exchange(copies, "dp"), "core").reshape(2, 16, 2, 8, 384)
+    tiles = lax.all_gather(exchange(copies, ("x", "y")), "core").reshape(2, 16, 2, 8, 384)
     left, right, new_memory = call(
         final_kernel,
         (shape(RANK, COLS), shape(RANK, COLS), shape(COLS, COLS)),
@@ -165,12 +173,12 @@
 
 def solution(mesh):
     replicas, pieces = mesh.devices.shape
-    split = Mesh(mesh.devices.reshape(replicas, pieces // 2, 2), ("dp", "z", "core"))
-    tensor = ("z", "core")
+    split = Mesh(mesh.devices.reshape(4, replicas // 4, pieces // 2, 2), ("x", "y", "z", "core"))
+    dp, tensor = ("x", "y"), ("z", "core")
     return jax.shard_map(
         on_device,
         mesh=split,
-        in_specs=(P("dp", tensor), P(("dp", "z", "core"), None), P("dp", tensor, None), P()),
-        out_specs=(P(tensor, None), P(), P("dp", tensor, None)),
+        in_specs=(P(dp, tensor), P(dp + tensor, None), P(dp, tensor, None), P()),
+        out_specs=(P(tensor, None), P(), P(dp, tensor, None)),
         check_vma=False,
     )

time: 170 us -> 161 us (0.947)
  blocking collectives: 149 us -> 140 us
    all_to_all x5 -> x7, blocking collectives: 145 us -> 137 us  [exchange(): return lax.all_to_all(pieces, axis, 0, 0, tiled=False)]
where the time goes in v6:
time: 161 us; the launch traced here: 160 us
  blocking collectives  140 us (87%)
  Pallas kernels  13 us (8%)
  starting transfers between devices  4.43 us (3%)
    all_to_all x7, blocking collectives, exchange(): return lax.all_to_all(pieces, axis, 0, 0, tiled=False)  137 us
    pallas_call x1, Pallas kernels, on_device(): call(final_kernel, (shape(RANK, COLS), shape(RANK, COLS), shape(COLS, COL...  8.82 us
    ppermute x1, starting transfers between devices, on_device(): other = lax.ppermute(own, 'core', [(0, 1), (1, 0)])  4.43 us
  transfers between devices with their start and end apart: 1, of which 1 were waited for; matrix products, arithmetic and copies ran while one was open for 0% of the time, Pallas kernels for 1%

profile of v6, /device:TPU:1, one launch (start us, length us, event | category | flops | bytes accessed | tf_op | source)
XLA Modules:
  0.0 160.3 jit_solution(9157442734526321230)
XLA Ops:
  0.6 0.0 copy-start.1
  0.6 1.1 broadcast_in_dim.16
  1.7 0.0 copy-start
  1.7 42.2 %all_to_all.35.grads_ref = bf16[8,152,512]{2,1,0:T(8,128)(2,1)S(1)} all-to-all(bf16[8,152,512]{2,1,0:T(8,128)(2,1)S(1)} %broadcast_in_dim.16), channel_id=1, replica_groups=mesh['x'=4,'y'=8,'z'=8,'core'=2] {'z'}, dimensions={0} | all-to-all | bytes 2490368 | tf_op jit(solution)/shard_map/all_to_all | solution.py:27
  43.9 4.4 %collective-permute-start = (bf16[8,152,512]{2,1,0:T(8,128)(2,1)S(1)}, bf16[8,152,512]{2,1,0:T(8,128)(2,1)S(1)}, u32[]{:S(2)}, u32[]{:S(2)}) collective-permute-start(bf16[8,152,512]{2,1,0:T(8,128)(2,1)S(1)} %all_to_all.35.grads_ref), channel_id=1, source_target_pairs={{0,1},{1,0},{2,3},{3,2},{4,5},{5,4},{6,7},{7,6},{8,9},{9,8},{10,11... | collective-permute-start | bytes 3735560 | tf_op jit(solution)/shard_map/ppermute | solution.py:149
  48.3 0.0 copy-done.1
  48.3 0.0 copy-done
  48.4 1.3 shard_map.67.start_ref
  49.7 1.2 collective-permute-done.grads_ref
  50.9 1.3 shard_map.68.merged_ref
  52.2 18.0 %all_to_all.36.parts_ref = f32[4,128,512]{2,1,0:T(8,128)S(1)} all-to-all(f32[4,128,512]{2,1,0:T(8,128)S(1)} %bitcast.15), channel_id=1, replica_groups=mesh['x'=4,'y'=8,'z'=8,'core'=2] {'x'}, dimensions={0} | all-to-all | bytes 2097152 | tf_op jit(solution)/shard_map/all_to_all | solution.py:27
  70.3 15.9 %all_to_all.37.parts_ref = f32[8,16,512]{2,1,0:T(8,128)S(1)} all-to-all(f32[8,16,512]{2,1,0:T(8,128)S(1)} %bitcast.17), channel_id=1, replica_groups=mesh['x'=4,'y'=8,'z'=8,'core'=2] {'y'}, dimensions={0} | all-to-all | bytes 524288 | tf_op jit(solution)/shard_map/all_to_all | solution.py:27
  86.2 11.9 %all_to_all.38 = f32[8,16,512]{2,1,0:T(8,128)S(1)} all-to-all(f32[8,16,512]{2,1,0:T(8,128)S(1)} %shard_map.70), channel_id=1, replica_groups=mesh['x'=4,'y'=8,'z'=8,'core'=2] {'y'}, dimensions={0} | all-to-all | bytes 524288 | tf_op jit(solution)/shard_map/all_to_all | solution.py:27
  98.1 0.1 broadcast_in_dim.18
  98.2 13.0 %all_to_all.39 = f32[4,128,512]{2,1,0:T(8,128)S(1)} all-to-all(f32[4,128,512]{2,1,0:T(8,128)S(1)} %broadcast_in_dim.18), channel_id=1, replica_groups=mesh['x'=4,'y'=8,'z'=8,'core'=2] {'x'}, dimensions={0} | all-to-all | bytes 2097152 | tf_op jit(solution)/shard_map/all_to_all | solution.py:27
  111.2 1.5 shard_map.71
  112.7 18.3 %all_to_all.40.parts_ref = f32[16,8,384]{2,1,0:T(8,128)S(1)} all-to-all(f32[16,8,384]{2,1,0:T(8,128)S(1)} %shard_map.71), channel_id=1, replica_groups=mesh['x'=4,'y'=8,'z'=8,'core'=2] {'z','core'}, dimensions={0} | all-to-all | bytes 393216 | tf_op jit(solution)/shard_map/all_to_all | solution.py:27
  131.0 0.0 copy-start.2
  131.0 17.5 %all_to_all.41 = f32[32,8,384]{2,1,0:T(8,128)S(1)} all-to-all(f32[32,8,384]{2,1,0:T(8,128)S(1)} %shard_map.72), channel_id=1, replica_groups=mesh['x'=4,'y'=8,'z'=8,'core'=2] {'x','y'}, dimensions={0} | all-to-all | bytes 786432 | tf_op jit(solution)/shard_map/all_to_all | solution.py:27
  148.5 2.9 %all-gather = f32[64,8,384]{2,1,0:T(8,128)S(1)} all-gather(f32[32,8,384]{2,1,0:T(8,128)S(1)} %all_to_all.41), channel_id=2, replica_groups=mesh['x'=4,'y'=8,'z'=8,'core'=2] {'core'}, dimensions={0}, use_global_device_ids=true | all-gather | bytes 1179648 | tf_op jit(solution)/shard_map/all_gather | solution.py:163
  151.5 0.0 copy-done.2
  151.5 8.8 %shard_map.73 = (f32[64,512]{1,0:T(8,128)}, f32[64,512]{1,0:T(8,128)}, f32[512,512]{1,0:T(8,128)}) custom-call(f32[2,16,2,8,384]{4,3,2,1,0:T(8,128)S(1)} %bitcast.16, f32[512,512]{1,0:T(8,128)S(1)} %bitcast.14, f32[512,512]{1,0:T(8,128)S(1)} %shard_map.68.merged_ref, f32[64,512]{1,0:T(8,128)S(1)} %bitcast.19), custom_call_target="tpu_custom_call" | custom-call | flops 268435456 | bytes 4194304 | tf_op jit(solution)/shard_map/pallas_call | solution.py:164
  (3 shorter events, 0.1 us)
Async XLA Ops:
  0.6 47.7 %copy-start.1 = (f32[1,512,512]{2,1,0:T(8,128)S(1)}, f32[1,512,512]{2,1,0:T(8,128)}, u32[]{:S(2)}) copy-start(f32[1,512,512]{2,1,0:T(8,128)} %param.6) | copy-start | bytes 3145732
  1.7 46.6 %copy-start = (bf16[2432,512]{1,0:T(8,128)(2,1)S(1)}, bf16[2432,512]{1,0:T(8,128)(2,1)}, u32[]{:S(2)}) copy-start(bf16[2432,512]{1,0:T(8,128)(2,1)} %param.4) | copy-start | bytes 7471108
  43.9 7.0 %collective-permute-start = (bf16[8,152,512]{2,1,0:T(8,128)(2,1)S(1)}, bf16[8,152,512]{2,1,0:T(8,128)(2,1)S(1)}, u32[]{:S(2)}, u32[]{:S(2)}) collective-permute-start(bf16[8,152,512]{2,1,0:T(8,128)(2,1)S(1)} %all_to_all.35.grads_ref), channel_id=1, source_target_pairs={{0,1},{1,0},{2,3},{3,2},{4,5},{5,4},{6,7},{7,6},{8,9},{9,8},{10,11... | collective-permute-start | bytes 3735560 | tf_op jit(solution)/shard_map/ppermute | solution.py:149
  131.0 20.5 %copy-start.2 = (f32[512,64]{0,1:T(8,128)S(1)}, f32[512,64]{0,1:T(8,128)}, u32[]{:S(2)}) copy-start(f32[512,64]{0,1:T(8,128)} %param.7) | copy-start | bytes 393220

commit v7 on v6

--- a/solution.py
+++ b/solution.py
@@ -17,6 +17,18 @@
     return lax.dot_general(
         a, b, (((ca,), (cb,)), ((), ())), precision=lax.Precision.HIGHEST, preferred_element_type=F32
     )
+
+
+def dot3(a, b, ca, cb):
+    def halves(v):
+        high = v.astype(jnp.bfloat16)
+        return high, (v - high.astype(F32)).astype(jnp.bfloat16)
+
+    def one(x, y):
+        return lax.dot_general(x, y, (((ca,), (cb,)), ((), ())), preferred_element_type=F32)
+
+    (ah, al), (bh, bl) = halves(a), halves(b)
+    return one(ah, bh) + (one(ah, bl) + one(al, bh))
 
 
 def shape(*dims):
@@ -50,12 +62,12 @@
 def moment_kernel(slab_ref, copies_ref):
     position = lax.axis_index("x") * lax.axis_size("y") + lax.axis_index("y")
     high = lax.rem(position, 2) == 1
-    first = jnp.where(high, 256, 0) + 8 * lax.div(position, 2)
-    step = lax.broadcasted_iota(jnp.int32, (16, COLS), 0)
-    wanted = step + jnp.where(step < 8, first, first + 120)
-    pick = jnp.where(lax.broadcasted_iota(jnp.int32, (16, COLS), 1) == wanted, 1.0, 0.0)
+    back = lax.rem(128 - 8 * lax.div(position, 2), 128)
     slab = slab_ref[...]
-    rows = dot(dot(pick, slab, 1, 1), slab, 1, 0)
+    even = pltpu.roll(jnp.where(high, slab[:, 256:384], slab[:, :128]), back, 1)
+    odd = pltpu.roll(jnp.where(high, slab[:, 384:], slab[:, 128:256]), lax.rem(back + 8, 128), 1)
+    lane = lax.broadcasted_iota(jnp.int32, (COLS, 128), 1)
+    rows = dot(jnp.where(lane < 8, even, odd).T[:16], slab, 1, 0)
     for core, row in enumerate((rows[:8], rows[8:])):
         turned = jnp.concatenate([row, row], axis=1)
         near = turned[:, 128 * core : 128 * core + 384]
@@ -121,13 +133,13 @@
     image = dot(start, moment[...], 1, 0)
     right = dot(inverse_factor(dot(start, image, 1, 1)), image, 1, 0)
     image = dot(right, moment[...], 1, 0)
-    left_raw = dot(right, slab_ref[...], 1, 1)
+    left_raw = dot3(right, slab_ref[...], 1, 1)
     inverse = inverse_factor(dot(right, image, 1, 1))
     left = dot(inverse, left_raw, 1, 0)
     right = dot(inverse, image, 1, 0)
     left_out[...] = math.sqrt(ROWS) * left
     right_out[...] = right
-    memory_out[...] = merged_ref[...] - dot(left, right, 0, 0)
+    memory_out[...] = merged_ref[...] - dot3(left, right, 0, 0)
 
 
 def call(kernel, out_shape, flops, moved, scratch=()):

time: 161 us -> 159 us (0.988)
  no operation moved by 1% of the time
where the time goes in v7:
time: 159 us
  blocking collectives  140 us (88%)
  Pallas kernels  11.5 us (7%)
  starting transfers between devices  4.43 us (3%)
    all_to_all x7, blocking collectives, exchange(): return lax.all_to_all(pieces, axis, 0, 0, tiled=False)  137 us
    pallas_call x1, Pallas kernels, on_device(): call(final_kernel, (shape(RANK, COLS), shape(RANK, COLS), shape(COLS, COL...  8 us
    ppermute x1, starting transfers between devices, on_device(): other = lax.ppermute(own, 'core', [(0, 1), (1, 0)])  4.43 us
  transfers between devices with their start and end apart: 1, of which 1 were waited for; matrix products, arithmetic and copies ran while one was open for 0% of the time, Pallas kernels for 1%

profile of v7, /device:TPU:1, one launch (start us, length us, event | category | flops | bytes accessed | tf_op | source)
XLA Modules:
  0.0 158.8 jit_solution(2801595930740137494)
XLA Ops:
  0.6 0.0 copy-start.1
  0.6 1.1 broadcast_in_dim.16
  1.7 0.0 copy-start
  1.7 42.2 %all_to_all.35.grads_ref = bf16[8,152,512]{2,1,0:T(8,128)(2,1)S(1)} all-to-all(bf16[8,152,512]{2,1,0:T(8,128)(2,1)S(1)} %broadcast_in_dim.16), channel_id=1, replica_groups=mesh['x'=4,'y'=8,'z'=8,'core'=2] {'z'}, dimensions={0} | all-to-all | bytes 2490368 | tf_op jit(solution)/shard_map/all_to_all | solution.py:39
  43.9 4.4 %collective-permute-start = (bf16[8,152,512]{2,1,0:T(8,128)(2,1)S(1)}, bf16[8,152,512]{2,1,0:T(8,128)(2,1)S(1)}, u32[]{:S(2)}, u32[]{:S(2)}) collective-permute-start(bf16[8,152,512]{2,1,0:T(8,128)(2,1)S(1)} %all_to_all.35.grads_ref), channel_id=1, source_target_pairs={{0,1},{1,0},{2,3},{3,2},{4,5},{5,4},{6,7},{7,6},{8,9},{9,8},{10,11... | collective-permute-start | bytes 3735560 | tf_op jit(solution)/shard_map/ppermute | solution.py:161
  48.3 0.0 copy-done.1
  48.3 0.0 copy-done
  48.4 1.3 shard_map.67.start_ref
  49.7 1.2 collective-permute-done.grads_ref
  50.9 1.3 shard_map.68.merged_ref
  52.2 18.0 %all_to_all.36.parts_ref = f32[4,128,512]{2,1,0:T(8,128)S(1)} all-to-all(f32[4,128,512]{2,1,0:T(8,128)S(1)} %bitcast.15), channel_id=1, replica_groups=mesh['x'=4,'y'=8,'z'=8,'core'=2] {'x'}, dimensions={0} | all-to-all | bytes 2097152 | tf_op jit(solution)/shard_map/all_to_all | solution.py:39
  70.3 15.9 %all_to_all.37.parts_ref = f32[8,16,512]{2,1,0:T(8,128)S(1)} all-to-all(f32[8,16,512]{2,1,0:T(8,128)S(1)} %bitcast.17), channel_id=1, replica_groups=mesh['x'=4,'y'=8,'z'=8,'core'=2] {'y'}, dimensions={0} | all-to-all | bytes 524288 | tf_op jit(solution)/shard_map/all_to_all | solution.py:39
  86.2 11.9 %all_to_all.38 = f32[8,16,512]{2,1,0:T(8,128)S(1)} all-to-all(f32[8,16,512]{2,1,0:T(8,128)S(1)} %shard_map.70), channel_id=1, replica_groups=mesh['x'=4,'y'=8,'z'=8,'core'=2] {'y'}, dimensions={0} | all-to-all | bytes 524288 | tf_op jit(solution)/shard_map/all_to_all | solution.py:39
  98.1 0.1 broadcast_in_dim.18
  98.2 13.0 %all_to_all.39 = f32[4,128,512]{2,1,0:T(8,128)S(1)} all-to-all(f32[4,128,512]{2,1,0:T(8,128)S(1)} %broadcast_in_dim.18), channel_id=1, replica_groups=mesh['x'=4,'y'=8,'z'=8,'core'=2] {'x'}, dimensions={0} | all-to-all | bytes 2097152 | tf_op jit(solution)/shard_map/all_to_all | solution.py:39
  111.2 0.7 shard_map.71
  112.0 18.3 %all_to_all.40.parts_ref = f32[16,8,384]{2,1,0:T(8,128)S(1)} all-to-all(f32[16,8,384]{2,1,0:T(8,128)S(1)} %shard_map.71), channel_id=1, replica_groups=mesh['x'=4,'y'=8,'z'=8,'core'=2] {'z','core'}, dimensions={0} | all-to-all | bytes 393216 | tf_op jit(solution)/shard_map/all_to_all | solution.py:39
  130.2 0.0 copy-start.2
  130.3 17.5 %all_to_all.41 = f32[32,8,384]{2,1,0:T(8,128)S(1)} all-to-all(f32[32,8,384]{2,1,0:T(8,128)S(1)} %shard_map.72), channel_id=1, replica_groups=mesh['x'=4,'y'=8,'z'=8,'core'=2] {'x','y'}, dimensions={0} | all-to-all | bytes 786432 | tf_op jit(solution)/shard_map/all_to_all | solution.py:39
  147.8 2.9 %all-gather = f32[64,8,384]{2,1,0:T(8,128)S(1)} all-gather(f32[32,8,384]{2,1,0:T(8,128)S(1)} %all_to_all.41), channel_id=2, replica_groups=mesh['x'=4,'y'=8,'z'=8,'core'=2] {'core'}, dimensions={0}, use_global_device_ids=true | all-gather | bytes 1179648 | tf_op jit(solution)/shard_map/all_gather | solution.py:175
  150.7 0.0 copy-done.2
  150.7 8.0 %shard_map.73 = (f32[64,512]{1,0:T(8,128)}, f32[64,512]{1,0:T(8,128)}, f32[512,512]{1,0:T(8,128)}) custom-call(f32[2,16,2,8,384]{4,3,2,1,0:T(8,128)S(1)} %bitcast.16, f32[512,512]{1,0:T(8,128)S(1)} %bitcast.14, f32[512,512]{1,0:T(8,128)S(1)} %shard_map.68.merged_ref, f32[64,512]{1,0:T(8,128)S(1)} %bitcast.19), custom_call_target="tpu_custom_call" | custom-call | flops 268435456 | bytes 4194304 | tf_op jit(solution)/shard_map/pallas_call | solution.py:176
  (3 shorter events, 0.1 us)
Async XLA Ops:
  0.6 47.7 %copy-start.1 = (f32[1,512,512]{2,1,0:T(8,128)S(1)}, f32[1,512,512]{2,1,0:T(8,128)}, u32[]{:S(2)}) copy-start(f32[1,512,512]{2,1,0:T(8,128)} %param.6) | copy-start | bytes 3145732
  1.7 46.6 %copy-start = (bf16[2432,512]{1,0:T(8,128)(2,1)S(1)}, bf16[2432,512]{1,0:T(8,128)(2,1)}, u32[]{:S(2)}) copy-start(bf16[2432,512]{1,0:T(8,128)(2,1)} %param.4) | copy-start | bytes 7471108
  43.9 7.0 %collective-permute-start = (bf16[8,152,512]{2,1,0:T(8,128)(2,1)S(1)}, bf16[8,152,512]{2,1,0:T(8,128)(2,1)S(1)}, u32[]{:S(2)}, u32[]{:S(2)}) collective-permute-start(bf16[8,152,512]{2,1,0:T(8,128)(2,1)S(1)} %all_to_all.35.grads_ref), channel_id=1, source_target_pairs={{0,1},{1,0},{2,3},{3,2},{4,5},{5,4},{6,7},{7,6},{8,9},{9,8},{10,11... | collective-permute-start | bytes 3735560 | tf_op jit(solution)/shard_map/ppermute | solution.py:161
  130.2 20.5 %copy-start.2 = (f32[512,64]{0,1:T(8,128)S(1)}, f32[512,64]{0,1:T(8,128)}, u32[]{:S(2)}) copy-start(f32[512,64]{0,1:T(8,128)} %param.7) | copy-start | bytes 393220

commit v8 on v7

--- a/solution.py
+++ b/solution.py
@@ -153,11 +153,12 @@
 
 
 def on_device(tokens_in, out_grad, memory, right_init):
-    replicas, layers = lax.axis_size(("x", "y")), lax.axis_size("z")
+    replicas, layers = lax.axis_size(("x", "y")), lax.axis_size(("zh", "zl"))
     rows = lax.axis_size("x")
     pieces = 2 * layers
     tokens = tokens_in.reshape(layers, 2, TOKENS, COLS)
-    own = exchange(jnp.broadcast_to(out_grad[None], (layers, TOKENS, COLS)), "z")
+    pair = exchange(jnp.broadcast_to(out_grad[None], (2, TOKENS, COLS)), "zl")
+    own = exchange(jnp.broadcast_to(pair[None], (layers // 2,) + pair.shape), "zh").reshape(layers, TOKENS, COLS)
     other = lax.ppermute(own, "core", [(0, 1), (1, 0)])
     half = call(functools.partial(gradient_kernel, 0), shape(COLS, COLS), 1 << 29, 1 << 22)
     merged = half(tokens, own, memory[0])
@@ -171,7 +172,7 @@
     part = exchange(copies, "y").reshape(COLS // rows, COLS)
     slab = exchange(jnp.broadcast_to(part[None], (rows,) + part.shape), "x").reshape(COLS, COLS)
     copies = call(moment_kernel, shape(pieces, 8, 384), 1 << 26, 1 << 20)(slab)
-    copies = call(sum_kernel, shape(replicas, 8, 384), 1 << 17, 1 << 20)(exchange(copies, ("z", "core")))
+    copies = call(sum_kernel, shape(replicas, 8, 384), 1 << 17, 1 << 20)(exchange(copies, ("zh", "zl", "core")))
     tiles = lax.all_gather(exchange(copies, ("x", "y")), "core").reshape(2, 16, 2, 8, 384)
     left, right, new_memory = call(
         final_kernel,
@@ -185,8 +186,8 @@
 
 def solution(mesh):
     replicas, pieces = mesh.devices.shape
-    split = Mesh(mesh.devices.reshape(4, replicas // 4, pieces // 2, 2), ("x", "y", "z", "core"))
-    dp, tensor = ("x", "y"), ("z", "core")
+    split = Mesh(mesh.devices.reshape(4, replicas // 4, pieces // 4, 2, 2), ("x", "y", "zh", "zl", "core"))
+    dp, tensor = ("x", "y"), ("zh", "zl", "core")
     return jax.shard_map(
         on_device,
         mesh=split,

time: 159 us -> 166 us (1.044)
  blocking collectives: 140 us -> 146 us
    all_to_all x7 -> x8, blocking collectives: 137 us -> 143 us  [exchange(): return lax.all_to_all(pieces, axis, 0, 0, tiled=False)]
where the time goes in v8:
time: 166 us; the launch traced here: 165 us
  blocking collectives  146 us (88%)
  Pallas kernels  11.5 us (7%)
  starting transfers between devices  4.45 us (3%)
    all_to_all x8, blocking collectives, exchange(): return lax.all_to_all(pieces, axis, 0, 0, tiled=False)  143 us
    pallas_call x1, Pallas kernels, on_device(): call(final_kernel, (shape(RANK, COLS), shape(RANK, COLS), shape(COLS, COL...  8 us
    ppermute x1, starting transfers between devices, on_device(): other = lax.ppermute(own, 'core', [(0, 1), (1, 0)])  4.45 us
  transfers between devices with their start and end apart: 1, of which 1 were waited for; matrix products, arithmetic and copies ran while one was open for 0% of the time, Pallas kernels for 1%

profile of v8, /device:TPU:1, one launch (start us, length us, event | category | flops | bytes accessed | tf_op | source)
XLA Modules:
  0.0 165.2 jit_solution(14913821082957195543)
XLA Ops:
  0.6 0.9 broadcast_in_dim.10
  1.6 8.3 %all_to_all.40 = bf16[2,152,512]{2,1,0:T(8,128)(2,1)S(1)} all-to-all(bf16[2,152,512]{2,1,0:T(8,128)(2,1)S(1)} %broadcast_in_dim.10), channel_id=1, replica_groups=mesh['x'=4,'y'=8,'zh'=4,'zl'=2,'core'=2] {'zl'}, dimensions={0} | all-to-all | bytes 622592 | tf_op jit(solution)/shard_map/all_to_all | solution.py:39
  9.8 0.0 copy-start.1
  9.8 0.1 broadcast_in_dim.11
  10.0 0.0 copy-start
  10.0 40.2 %all_to_all.41 = bf16[4,2,152,512]{3,2,1,0:T(8,128)(2,1)S(1)} all-to-all(bf16[4,2,152,512]{3,2,1,0:T(8,128)(2,1)S(1)} %broadcast_in_dim.11), channel_id=1, replica_groups=mesh['x'=4,'y'=8,'zh'=4,'zl'=2,'core'=2] {'zh'}, dimensions={0} | all-to-all | bytes 2490368 | tf_op jit(solution)/shard_map/all_to_all | solution.py:39
  50.2 4.5 %collective-permute-start = (bf16[8,152,512]{2,1,0:T(8,128)(2,1)S(1)}, bf16[8,152,512]{2,1,0:T(8,128)(2,1)S(1)}, u32[]{:S(2)}, u32[]{:S(2)}) collective-permute-start(bf16[8,152,512]{2,1,0:T(8,128)(2,1)S(1)} %bitcast.17), channel_id=1, source_target_pairs={{0,1},{1,0},{2,3},{3,2},{4,5},{5,4},{6,7},{7,6},{8,9},{9,8},{10,11... | collective-permute-start | bytes 3735560 | tf_op jit(solution)/shard_map/ppermute | solution.py:162
  54.6 0.0 copy-done.1
  54.7 0.0 copy-done
  54.7 1.3 shard_map.67.start_ref
  56.0 1.2 collective-permute-done.grads_ref
  57.2 1.3 shard_map.68.merged_ref
  58.5 18.1 %all_to_all.42.parts_ref = f32[4,128,512]{2,1,0:T(8,128)S(1)} all-to-all(f32[4,128,512]{2,1,0:T(8,128)S(1)} %bitcast.16), channel_id=1, replica_groups=mesh['x'=4,'y'=8,'zh'=4,'zl'=2,'core'=2] {'x'}, dimensions={0} | all-to-all | bytes 2097152 | tf_op jit(solution)/shard_map/all_to_all | solution.py:39
  76.6 15.8 %all_to_all.43.parts_ref = f32[8,16,512]{2,1,0:T(8,128)S(1)} all-to-all(f32[8,16,512]{2,1,0:T(8,128)S(1)} %bitcast.20), channel_id=1, replica_groups=mesh['x'=4,'y'=8,'zh'=4,'zl'=2,'core'=2] {'y'}, dimensions={0} | all-to-all | bytes 524288 | tf_op jit(solution)/shard_map/all_to_all | solution.py:39
  92.5 11.9 %all_to_all.44 = f32[8,16,512]{2,1,0:T(8,128)S(1)} all-to-all(f32[8,16,512]{2,1,0:T(8,128)S(1)} %shard_map.70), channel_id=1, replica_groups=mesh['x'=4,'y'=8,'zh'=4,'zl'=2,'core'=2] {'y'}, dimensions={0} | all-to-all | bytes 524288 | tf_op jit(solution)/shard_map/all_to_all | solution.py:39
  104.4 0.1 broadcast_in_dim.25
  104.5 13.0 %all_to_all.45 = f32[4,128,512]{2,1,0:T(8,128)S(1)} all-to-all(f32[4,128,512]{2,1,0:T(8,128)S(1)} %broadcast_in_dim.25), channel_id=1, replica_groups=mesh['x'=4,'y'=8,'zh'=4,'zl'=2,'core'=2] {'x'}, dimensions={0} | all-to-all | bytes 2097152 | tf_op jit(solution)/shard_map/all_to_all | solution.py:39
  117.4 0.7 shard_map.71
  118.2 18.6 %all_to_all.46.parts_ref = f32[16,8,384]{2,1,0:T(8,128)S(1)} all-to-all(f32[16,8,384]{2,1,0:T(8,128)S(1)} %shard_map.71), channel_id=1, replica_groups=mesh['x'=4,'y'=8,'zh'=4,'zl'=2,'core'=2] {'zh','zl','core'}, dimensions={0} | all-to-all | bytes 393216 | tf_op jit(solution)/shard_map/all_to_all | solution.py:39
  136.8 0.0 copy-start.2
  136.8 17.4 %all_to_all.47 = f32[32,8,384]{2,1,0:T(8,128)S(1)} all-to-all(f32[32,8,384]{2,1,0:T(8,128)S(1)} %shard_map.72), channel_id=1, replica_groups=mesh['x'=4,'y'=8,'zh'=4,'zl'=2,'core'=2] {'x','y'}, dimensions={0} | all-to-all | bytes 786432 | tf_op jit(solution)/shard_map/all_to_all | solution.py:39
  154.2 3.0 %all-gather = f32[64,8,384]{2,1,0:T(8,128)S(1)} all-gather(f32[32,8,384]{2,1,0:T(8,128)S(1)} %all_to_all.47), channel_id=2, replica_groups=mesh['x'=4,'y'=8,'zh'=4,'zl'=2,'core'=2] {'core'}, dimensions={0}, use_global_device_ids=true | all-gather | bytes 1179648 | tf_op jit(solution)/shard_map/all_gather | solution.py:176
  157.2 0.0 copy-done.2
  157.2 8.0 %shard_map.73 = (f32[64,512]{1,0:T(8,128)}, f32[64,512]{1,0:T(8,128)}, f32[512,512]{1,0:T(8,128)}) custom-call(f32[2,16,2,8,384]{4,3,2,1,0:T(8,128)S(1)} %bitcast.19, f32[512,512]{1,0:T(8,128)S(1)} %bitcast.15, f32[512,512]{1,0:T(8,128)S(1)} %shard_map.68.merged_ref, f32[64,512]{1,0:T(8,128)S(1)} %bitcast.22), custom_call_target="tpu_custom_call" | custom-call | flops 268435456 | bytes 4194304 | tf_op jit(solution)/shard_map/pallas_call | solution.py:177
  (3 shorter events, 0.1 us)
Async XLA Ops:
  9.8 44.8 %copy-start.1 = (f32[1,512,512]{2,1,0:T(8,128)S(1)}, f32[1,512,512]{2,1,0:T(8,128)}, u32[]{:S(2)}) copy-start(f32[1,512,512]{2,1,0:T(8,128)} %param.6) | copy-start | bytes 3145732
  10.0 44.7 %copy-start = (bf16[2432,512]{1,0:T(8,128)(2,1)S(1)}, bf16[2432,512]{1,0:T(8,128)(2,1)}, u32[]{:S(2)}) copy-start(bf16[2432,512]{1,0:T(8,128)(2,1)} %param.4) | copy-start | bytes 7471108
  50.2 7.0 %collective-permute-start = (bf16[8,152,512]{2,1,0:T(8,128)(2,1)S(1)}, bf16[8,152,512]{2,1,0:T(8,128)(2,1)S(1)}, u32[]{:S(2)}, u32[]{:S(2)}) collective-permute-start(bf16[8,152,512]{2,1,0:T(8,128)(2,1)S(1)} %bitcast.17), channel_id=1, source_target_pairs={{0,1},{1,0},{2,3},{3,2},{4,5},{5,4},{6,7},{7,6},{8,9},{9,8},{10,11... | collective-permute-start | bytes 3735560 | tf_op jit(solution)/shard_map/ppermute | solution.py:162
  136.8 20.5 %copy-start.2 = (f32[512,64]{0,1:T(8,128)S(1)}, f32[512,64]{0,1:T(8,128)}, u32[]{:S(2)}) copy-start(f32[512,64]{0,1:T(8,128)} %param.7) | copy-start | bytes 393220

commit v9 on v7

--- a/solution.py
+++ b/solution.py
@@ -171,8 +171,11 @@
     part = exchange(copies, "y").reshape(COLS // rows, COLS)
     slab = exchange(jnp.broadcast_to(part[None], (rows,) + part.shape), "x").reshape(COLS, COLS)
     copies = call(moment_kernel, shape(pieces, 8, 384), 1 << 26, 1 << 20)(slab)
-    copies = call(sum_kernel, shape(replicas, 8, 384), 1 << 17, 1 << 20)(exchange(copies, ("z", "core")))
-    tiles = lax.all_gather(exchange(copies, ("x", "y")), "core").reshape(2, 16, 2, 8, 384)
+    columns = replicas // rows
+    copies = call(sum_kernel, shape(columns, 8, 384), 1 << 17, 1 << 20)(exchange(copies, ("z", "core")))
+    part = exchange(copies, "y")
+    tiles = exchange(jnp.broadcast_to(part[None], (rows,) + part.shape), "x")
+    tiles = lax.all_gather(tiles.reshape(replicas, 8, 384), "core").reshape(2, 16, 2, 8, 384)
     left, right, new_memory = call(
         final_kernel,
         (shape(RANK, COLS), shape(RANK, COLS), shape(COLS, COLS)),

time: 159 us -> 164 us (1.031)
  blocking collectives: 140 us -> 144 us
    all_to_all x7 -> x8, blocking collectives: 137 us -> 141 us  [exchange(): return lax.all_to_all(pieces, axis, 0, 0, tiled=False)]
where the time goes in v9:
time: 164 us; the launch traced here: 163 us
  blocking collectives  144 us (88%)
  Pallas kernels  11.5 us (7%)
  starting transfers between devices  4.43 us (3%)
    all_to_all x8, blocking collectives, exchange(): return lax.all_to_all(pieces, axis, 0, 0, tiled=False)  141 us
    pallas_call x1, Pallas kernels, on_device(): call(final_kernel, (shape(RANK, COLS), shape(RANK, COLS), shape(COLS, COL...  8 us
    ppermute x1, starting transfers between devices, on_device(): other = lax.ppermute(own, 'core', [(0, 1), (1, 0)])  4.43 us
    all_gather x1, blocking collectives, on_device(): lax.all_gather(tiles.reshape(replicas, 8, 384), 'core')  3.34 us
  transfers between devices with their start and end apart: 1, of which 1 were waited for; matrix products, arithmetic and copies ran while one was open for 0% of the time, Pallas kernels for 1%

profile of v9, /device:TPU:1, one launch (start us, length us, event | category | flops | bytes accessed | tf_op | source)
XLA Modules:
  0.0 163.0 jit_solution(7193346671154141541)
XLA Ops:
  0.6 0.0 copy-start.1
  0.6 1.1 broadcast_in_dim.10
  1.7 0.0 copy-start
  1.7 42.2 %all_to_all.40.grads_ref = bf16[8,152,512]{2,1,0:T(8,128)(2,1)S(1)} all-to-all(bf16[8,152,512]{2,1,0:T(8,128)(2,1)S(1)} %broadcast_in_dim.10), channel_id=1, replica_groups=mesh['x'=4,'y'=8,'z'=8,'core'=2] {'z'}, dimensions={0} | all-to-all | bytes 2490368 | tf_op jit(solution)/shard_map/all_to_all | solution.py:39
  43.9 4.4 %collective-permute-start = (bf16[8,152,512]{2,1,0:T(8,128)(2,1)S(1)}, bf16[8,152,512]{2,1,0:T(8,128)(2,1)S(1)}, u32[]{:S(2)}, u32[]{:S(2)}) collective-permute-start(bf16[8,152,512]{2,1,0:T(8,128)(2,1)S(1)} %all_to_all.40.grads_ref), channel_id=1, source_target_pairs={{0,1},{1,0},{2,3},{3,2},{4,5},{5,4},{6,7},{7,6},{8,9},{9,8},{10,11... | collective-permute-start | bytes 3735560 | tf_op jit(solution)/shard_map/ppermute | solution.py:161
  48.3 0.0 copy-done.1
  48.3 0.0 copy-done
  48.4 1.3 shard_map.67.start_ref
  49.7 1.2 collective-permute-done.grads_ref
  50.9 1.3 shard_map.68.merged_ref
  52.2 18.0 %all_to_all.41.parts_ref = f32[4,128,512]{2,1,0:T(8,128)S(1)} all-to-all(f32[4,128,512]{2,1,0:T(8,128)S(1)} %bitcast.16), channel_id=1, replica_groups=mesh['x'=4,'y'=8,'z'=8,'core'=2] {'x'}, dimensions={0} | all-to-all | bytes 2097152 | tf_op jit(solution)/shard_map/all_to_all | solution.py:39
  70.3 15.9 %all_to_all.42.parts_ref = f32[8,16,512]{2,1,0:T(8,128)S(1)} all-to-all(f32[8,16,512]{2,1,0:T(8,128)S(1)} %bitcast.18), channel_id=1, replica_groups=mesh['x'=4,'y'=8,'z'=8,'core'=2] {'y'}, dimensions={0} | all-to-all | bytes 524288 | tf_op jit(solution)/shard_map/all_to_all | solution.py:39
  86.2 11.9 %all_to_all.43 = f32[8,16,512]{2,1,0:T(8,128)S(1)} all-to-all(f32[8,16,512]{2,1,0:T(8,128)S(1)} %shard_map.70), channel_id=1, replica_groups=mesh['x'=4,'y'=8,'z'=8,'core'=2] {'y'}, dimensions={0} | all-to-all | bytes 524288 | tf_op jit(solution)/shard_map/all_to_all | solution.py:39
  98.1 0.1 broadcast_in_dim.24
  98.2 13.0 %all_to_all.44 = f32[4,128,512]{2,1,0:T(8,128)S(1)} all-to-all(f32[4,128,512]{2,1,0:T(8,128)S(1)} %broadcast_in_dim.24), channel_id=1, replica_groups=mesh['x'=4,'y'=8,'z'=8,'core'=2] {'x'}, dimensions={0} | all-to-all | bytes 2097152 | tf_op jit(solution)/shard_map/all_to_all | solution.py:39
  111.2 0.7 shard_map.71
  112.0 18.3 %all_to_all.45.parts_ref = f32[16,8,384]{2,1,0:T(8,128)S(1)} all-to-all(f32[16,8,384]{2,1,0:T(8,128)S(1)} %shard_map.71), channel_id=1, replica_groups=mesh['x'=4,'y'=8,'z'=8,'core'=2] {'z','core'}, dimensions={0} | all-to-all | bytes 393216 | tf_op jit(solution)/shard_map/all_to_all | solution.py:39
  130.3 11.2 %all_to_all.46 = f32[8,8,384]{2,1,0:T(8,128)S(1)} all-to-all(f32[8,8,384]{2,1,0:T(8,128)S(1)} %shard_map.72), channel_id=1, replica_groups=mesh['x'=4,'y'=8,'z'=8,'core'=2] {'y'}, dimensions={0} | all-to-all | bytes 196608 | tf_op jit(solution)/shard_map/all_to_all | solution.py:39
  141.5 0.0 copy-start.2
  141.5 10.2 %all_to_all.47 = f32[4,8,8,384]{3,2,1,0:T(8,128)S(1)} all-to-all(f32[4,8,8,384]{3,2,1,0:T(8,128)S(1)} %broadcast_in_dim.25), channel_id=1, replica_groups=mesh['x'=4,'y'=8,'z'=8,'core'=2] {'x'}, dimensions={0} | all-to-all | bytes 786432 | tf_op jit(solution)/shard_map/all_to_all | solution.py:39
  151.7 3.3 %all_gather.3 = f32[2,32,8,384]{3,2,1,0:T(8,128)S(1)} all-gather(f32[1,32,8,384]{3,2,1,0:T(8,128)S(1)} %bitcast.21), channel_id=1, replica_groups=mesh['x'=4,'y'=8,'z'=8,'core'=2] {'core'}, dimensions={0}, use_global_device_ids=true | all-gather | bytes 1179648 | tf_op jit(solution)/shard_map/all_gather | solution.py:178
  155.0 0.0 copy-done.2
  155.0 8.0 %shard_map.73 = (f32[64,512]{1,0:T(8,128)}, f32[64,512]{1,0:T(8,128)}, f32[512,512]{1,0:T(8,128)}) custom-call(f32[2,16,2,8,384]{4,3,2,1,0:T(8,128)S(1)} %bitcast.17, f32[512,512]{1,0:T(8,128)S(1)} %bitcast.15, f32[512,512]{1,0:T(8,128)S(1)} %shard_map.68.merged_ref, f32[64,512]{1,0:T(8,128)S(1)} %bitcast.20), custom_call_target="tpu_custom_call" | custom-call | flops 268435456 | bytes 4194304 | tf_op jit(solution)/shard_map/pallas_call | solution.py:179
  (4 shorter events, 0.1 us)
Async XLA Ops:
  0.6 47.7 %copy-start.1 = (f32[1,512,512]{2,1,0:T(8,128)S(1)}, f32[1,512,512]{2,1,0:T(8,128)}, u32[]{:S(2)}) copy-start(f32[1,512,512]{2,1,0:T(8,128)} %param.6) | copy-start | bytes 3145732
  1.7 46.6 %copy-start = (bf16[2432,512]{1,0:T(8,128)(2,1)S(1)}, bf16[2432,512]{1,0:T(8,128)(2,1)}, u32[]{:S(2)}) copy-start(bf16[2432,512]{1,0:T(8,128)(2,1)} %param.4) | copy-start | bytes 7471108
  43.9 7.0 %collective-permute-start = (bf16[8,152,512]{2,1,0:T(8,128)(2,1)S(1)}, bf16[8,152,512]{2,1,0:T(8,128)(2,1)S(1)}, u32[]{:S(2)}, u32[]{:S(2)}) collective-permute-start(bf16[8,152,512]{2,1,0:T(8,128)(2,1)S(1)} %all_to_all.40.grads_ref), channel_id=1, source_target_pairs={{0,1},{1,0},{2,3},{3,2},{4,5},{5,4},{6,7},{7,6},{8,9},{9,8},{10,11... | collective-permute-start | bytes 3735560 | tf_op jit(solution)/shard_map/ppermute | solution.py:161
  141.5 13.6 %copy-start.2 = (f32[512,64]{0,1:T(8,128)S(1)}, f32[512,64]{0,1:T(8,128)}, u32[]{:S(2)}) copy-start(f32[512,64]{0,1:T(8,128)} %param.7) | copy-start | bytes 393220
